TPU v7x, 128 devices: a whole 4x4x4 slice. The times are simulated.
128 devices in a mesh: row: 8 (over y, z_lo), col: 16 (over z_hi, x, core).
Axes of the slice: x: 4, y: 4, z: 4 (z_hi: 2, z_lo: 2; z = z_hi * 2 + z_lo), core: 2. Of those that a mesh axis runs over, the one named last changes fastest.
Arguments:
- fire_state: float32 [64, 384, 2048], P(None, 'row', 'col'), may hold values from -6 to 6
- fuel_class: int32 [384, 2048], P('row', 'col'), may hold values from 0 to 12
- firebreak: int32 [384, 2048], P('row', 'col'), may hold values 0 or 1
- ignition: int32 [384, 2048], P('row', 'col'), may hold values 0 or 1
- spread_rate: float32 [13, 64], replicated, may hold values from 0.03 to 0.12
- spread_rows: float32 [64, 64], replicated, may hold values from -0.375 to 0.375
- spread_cols: float32 [64, 64], replicated, may hold values from -0.375 to 0.375
- reaction: float32 [64, 64], replicated, may hold values from -0.75 to 0.75
- ignition_heat: float32 [64], replicated, may hold values from -4 to 4
Outputs:
- final_state: float32 [64, 384, 2048], P(None, 'row', 'col')
All inputs are finite; a program needn't handle non-finite values. No bound on the sum of `firebreak` or of `ignition` on one device may be relied on, other than what follows from the above.
Results may differ from a plain program's by a relative error of at most 0.0003.
Values sent between devices are 32-bit elements; how exact they have to be, the bound alone decides.
No kernel may reach another device: no remote copies, remote signals or barrier semaphores. Data moves between devices by JAX's collectives and lax.ppermute only.
A program may use at most 64 MiB of HBM per device.

v0:
```python
import jax
import jax.numpy as jnp
from jax import lax
from jax.sharding import PartitionSpec as P

ITERS = 4


def with_halo(x, sides, width):
    edges = {}
    for axis, dim in sides:
        size, length = (lax.axis_size(axis), x.shape[dim])
        up = [(i, (i + 1) % size) for i in range(size - 1)]
        last = lax.slice_in_dim(x, length - width, length, axis=dim)
        leading = lax.slice_in_dim(x, 0, width, axis=dim)
        edges[dim] = (
            lax.ppermute(last, axis, up),
            lax.ppermute(leading, axis, [(b, a) for a, b in up]),
        )
    done = []
    for _, dim in sides:
        low, high = edges[dim]
        around = [(width, width) if d in done else (0, 0) for d in range(x.ndim)]
        x = jnp.concatenate([jnp.pad(low, around), x, jnp.pad(high, around)], axis=dim)
        done.append(dim)
    return x


def mixing(matrix, values):
    return jnp.einsum("dc,chw->dhw", matrix, values, precision=lax.Precision.HIGHEST)


def cell_terms(burnable_int, fuel_class, ignition, spread_rate, ignition_heat):
    burnable = burnable_int.astype(jnp.float32)
    classes = jnp.arange(spread_rate.shape[0], dtype=jnp.int32)
    onehot = (fuel_class[None] == classes[:, None, None]).astype(jnp.float32)
    spread = jnp.einsum("kc,khw->chw", spread_rate, onehot, precision=lax.Precision.HIGHEST)
    heating = ignition.astype(jnp.float32)[None] * ignition_heat[:, None, None]
    return (burnable, spread, heating)


def tendency(padded, terms, spread_rows, spread_cols, reaction):
    burnable, spread, heating = terms
    center = padded[:, 1:-1, 1:-1]
    vertical = padded[:, :-2, 1:-1] + padded[:, 2:, 1:-1] - 2.0 * center
    horizontal = padded[:, 1:-1, :-2] + padded[:, 1:-1, 2:] - 2.0 * center
    mixed = vertical + mixing(spread_rows, vertical) + horizontal + mixing(spread_cols, horizontal)
    drive = spread * mixed + mixing(reaction, jnp.tanh(center)) + heating
    return burnable[None] * drive - 0.5 * center


def edged(field):
    return with_halo(field, (("row", 1), ("col", 2)), 1)


def per_device(
    fire_state,
    fuel_class,
    firebreak,
    ignition,
    spread_rate,
    spread_rows,
    spread_cols,
    reaction,
    ignition_heat,
):
    burnable_int = 1 - firebreak
    field = fire_state
    terms = cell_terms(burnable_int, fuel_class, ignition, spread_rate, ignition_heat)
    for iteration in range(ITERS):
        first = tendency(edged(field), terms, spread_rows, spread_cols, reaction)
        middle = field + first
        second = tendency(edged(middle), terms, spread_rows, spread_cols, reaction)
        field = field + 0.5 * (first + second)
    return field


def solution(mesh):
    return jax.shard_map(
        per_device,
        mesh=mesh,
        in_specs=(
            P(None, "row", "col"),
            P("row", "col"),
            P("row", "col"),
            P("row", "col"),
            P(),
            P(),
            P(),
            P(),
            P(),
        ),
        out_specs=P(None, "row", "col"),
        check_vma=False,
    )
```

profile of v0, /device:TPU:15, one launch (start us, length us, event | category | flops | bytes accessed | tf_op | source)
XLA Modules:
  0.0 311.9 jit_solution(11037837349800146342)
XLA Ops:
  2.1 3.5 %collective-permute-start = (f32[64,1,128]{2,0,1:T(8,128)S(1)}, f32[64,1,128]{2,0,1:T(8,128)S(1)}, u32[]{:S(2)}, u32[]{:S(2)}) collective-permute-start(f32[64,1,128]{2,0,1:T(8,128)S(1)} %get-tuple-element.35), channel_id=1, source_target_pairs={{0,16},{16,32},{32,48},{48,64},{64,80},{80,96},{96,112},{1,17},{17... | collective-permute-start | bytes 98312 | tf_op jit(solution)/shard_map/ppermute | solution.py:17
  12.4 3.1 %collective-permute-start.3 = (f32[64,48,1]{0,1,2:T(8,128)S(1)}, f32[64,48,1]{0,1,2:T(8,128)S(1)}, u32[]{:S(2)}, u32[]{:S(2)}) collective-permute-start(f32[64,48,1]{0,1,2:T(8,128)S(1)} %copy.67), channel_id=1, source_target_pairs={{1,0},{2,1},{3,2},{4,3},{5,4},{6,5},{7,6},{8,7},{9,8},{10,9},{11,1... | collective-permute-start | bytes 36872 | tf_op jit(solution)/shard_map/ppermute | solution.py:18
  17.6 6.4 %collective-permute-start.2 = (f32[64,48,1]{0,1,2:T(8,128)S(1)}, f32[64,48,1]{0,1,2:T(8,128)S(1)}, u32[]{:S(2)}, u32[]{:S(2)}) collective-permute-start(f32[64,48,1]{0,1,2:T(8,128)S(1)} %copy.66), channel_id=1, source_target_pairs={{0,1},{1,2},{2,3},{3,4},{4,5},{5,6},{6,7},{7,8},{8,9},{9,10},{10,1... | collective-permute-start | bytes 36872 | tf_op jit(solution)/shard_map/ppermute | solution.py:17
  26.3 3.0 fusion.94
  35.7 8.3 %copy_add_fusion = (f32[64,48,128]{2,0,1:T(8,128)S(1)}, f32[64,48,128]{2,0,1:T(8,128)}) fusion(f32[64,48,128]{2,1,0:T(8,128)S(1)} %copy-done.1, f32[64,48,128]{2,0,1:T(8,128)} %copy-done.6, f32[64]{0:T(128)S(1)} %copy-done.38, f32[48,128]{1,0:T(8,128)S(1)} %convert_element_type.25, f32[64,48,128]{2,0,1:T(8,128)S(1)} %copy-done.17, ...), kind=kOutput, calls=%fused_computation.321 | convolution fusion | flops 316538880 | bytes 12804352 | tf_op jit(solution)/shard_map/dc,chw->dhw/dot_general | solution.py:30
  46.6 3.5 %collective-permute-start.5 = (f32[64,1,128]{2,0,1:T(8,128)S(1)}, f32[64,1,128]{2,0,1:T(8,128)S(1)}, u32[]{:S(2)}, u32[]{:S(2)}) collective-permute-start(f32[64,1,128]{2,0,1:T(8,128)S(1)} %get-tuple-element.32), channel_id=1, source_target_pairs={{16,0},{32,16},{48,32},{64,48},{80,64},{96,80},{112,96},{17,1},{33... | collective-permute-start | bytes 98312 | tf_op jit(solution)/shard_map/ppermute | solution.py:18
  54.3 3.8 %collective-permute-start.6 = (f32[64,48,1]{0,1,2:T(8,128)S(1)}, f32[64,48,1]{0,1,2:T(8,128)S(1)}, u32[]{:S(2)}, u32[]{:S(2)}) collective-permute-start(f32[64,48,1]{0,1,2:T(8,128)S(1)} %copy.36), channel_id=1, source_target_pairs={{0,1},{1,2},{2,3},{3,4},{4,5},{5,6},{6,7},{7,8},{8,9},{9,10},{10,1... | collective-permute-start | bytes 36872 | tf_op jit(solution)/shard_map/ppermute | solution.py:17
  64.2 4.6 %collective-permute-done.7 = f32[64,48,1]{0,1,2:T(8,128)S(1)} collective-permute-done((f32[64,48,1]{0,1,2:T(8,128)S(1)}, f32[64,48,1]{0,1,2:T(8,128)S(1)}, u32[]{:S(2)}, u32[]{:S(2)}) %collective-permute-start.7) | collective-permute-done | bytes 12320 | tf_op jit(solution)/shard_map/ppermute | solution.py:18
  75.0 3.6 %fusion.6 = f32[64,48,128]{2,0,1:T(8,128)S(1)} fusion(f32[64,48,128]{2,0,1:T(8,128)S(1)} %copy-done.18, f32[48,128,64]{1,2,0:T(8,128)S(1)} %fusion.189, f32[48,128,64]{1,2,0:T(8,128)S(1)} %fusion.137, f32[48,128,64]{1,2,0:T(8,128)S(1)} %copy-done.10, f32[64,48,128]{2,0,1:T(8,128)S(1)} %get-tuple-element.37, f32[64,1,128]{2,0,1:T(8,128)S(1)} %collective-permute-done.5, ...), kind=kOutput, calls=%fused_computation.14 | convolution fusion | flops 314572800 | bytes 11165952 | tf_op jit(solution)/shard_map/dc,chw->dhw/dot_general | solution.py:30
  82.3 4.3 %collective-permute-start.9 = (f32[64,1,128]{2,0,1:T(8,128)S(1)}, f32[64,1,128]{2,0,1:T(8,128)S(1)}, u32[]{:S(2)}, u32[]{:S(2)}) collective-permute-start(f32[64,1,128]{2,0,1:T(8,128)S(1)} %get-tuple-element.28), channel_id=1, source_target_pairs={{16,0},{32,16},{48,32},{64,48},{80,64},{96,80},{112,96},{17,1},{33... | collective-permute-start | bytes 98312 | tf_op jit(solution)/shard_map/ppermute | solution.py:18
  91.1 7.4 %collective-permute-start.10 = (f32[64,48,1]{0,1,2:T(8,128)S(1)}, f32[64,48,1]{0,1,2:T(8,128)S(1)}, u32[]{:S(2)}, u32[]{:S(2)}) collective-permute-start(f32[64,48,1]{0,1,2:T(8,128)S(1)} %copy.41), channel_id=1, source_target_pairs={{0,1},{1,2},{2,3},{3,4},{4,5},{5,6},{6,7},{7,8},{8,9},{9,10},{10,1... | collective-permute-start | bytes 36872 | tf_op jit(solution)/shard_map/ppermute | solution.py:17
  98.5 2.8 fusion.112
  106.7 9.0 %fusion.86 = (f32[64,48,128]{2,0,1:T(8,128)S(1)}, f32[64,48,128]{2,0,1:T(8,128)}) fusion(f32[64,48,128]{2,0,1:T(8,128)S(1)} %copy-done.3, f32[48,128,64]{1,2,0:T(8,128)S(1)} %copy-done.21, f32[64]{0:T(128)S(1)} %copy-done.38, f32[48,128]{1,0:T(8,128)S(1)} %convert_element_type.25, f32[48,128]{1,0:T(8,128)S(1)} %subtract_convert_fusion, ...), kind=kOutput, calls=%fused_computation.174 | convolution fusion | flops 319684608 | bytes 9593088 | tf_op jit(solution)/shard_map/dc,chw->dhw/dot_general | solution.py:30
  117.7 4.1 %collective-permute-start.13 = (f32[64,1,128]{2,0,1:T(8,128)S(1)}, f32[64,1,128]{2,0,1:T(8,128)S(1)}, u32[]{:S(2)}, u32[]{:S(2)}) collective-permute-start(f32[64,1,128]{2,0,1:T(8,128)S(1)} %get-tuple-element.24), channel_id=1, source_target_pairs={{16,0},{32,16},{48,32},{64,48},{80,64},{96,80},{112,96},{17,1},{33... | collective-permute-start | bytes 98312 | tf_op jit(solution)/shard_map/ppermute | solution.py:18
  126.0 6.3 %collective-permute-start.14 = (f32[64,48,1]{0,1,2:T(8,128)S(1)}, f32[64,48,1]{0,1,2:T(8,128)S(1)}, u32[]{:S(2)}, u32[]{:S(2)}) collective-permute-start(f32[64,48,1]{0,1,2:T(8,128)S(1)} %copy.45), channel_id=1, source_target_pairs={{0,1},{1,2},{2,3},{3,4},{4,5},{5,6},{6,7},{7,8},{8,9},{9,10},{10,1... | collective-permute-start | bytes 36872 | tf_op jit(solution)/shard_map/ppermute | solution.py:17
  138.2 4.8 %collective-permute-done.15 = f32[64,48,1]{0,1,2:T(8,128)S(1)} collective-permute-done((f32[64,48,1]{0,1,2:T(8,128)S(1)}, f32[64,48,1]{0,1,2:T(8,128)S(1)}, u32[]{:S(2)}, u32[]{:S(2)}) %collective-permute-start.15) | collective-permute-done | bytes 12320 | tf_op jit(solution)/shard_map/ppermute | solution.py:18
  149.2 7.6 %fusion.13 = f32[64,48,128]{2,0,1:T(8,128)S(1)} fusion(f32[64,48,128]{2,0,1:T(8,128)S(1)} %copy-done.3, f32[48,128,64]{1,2,0:T(8,128)S(1)} %fusion.186, f32[48,128,64]{1,2,0:T(8,128)S(1)} %fusion.132, f32[64,48,128]{2,0,1:T(8,128)S(1)} %copy-done.41, f32[48,128,64]{1,2,0:T(8,128)S(1)} %copy-done.22, f32[48,128,64]{1,2,0:T(8,128)S(1)} %copy-done.12, ...), kind=kOutput, calls=%fused_computation.21 | convolution fusion | flops 316538880 | bytes 12738816 | tf_op jit(solution)/shard_map/dc,chw->dhw/dot_general | solution.py:30
  160.6 4.3 %collective-permute-start.17 = (f32[64,1,128]{2,0,1:T(8,128)S(1)}, f32[64,1,128]{2,0,1:T(8,128)S(1)}, u32[]{:S(2)}, u32[]{:S(2)}) collective-permute-start(f32[64,1,128]{2,0,1:T(8,128)S(1)} %get-tuple-element.20), channel_id=1, source_target_pairs={{16,0},{32,16},{48,32},{64,48},{80,64},{96,80},{112,96},{17,1},{33... | collective-permute-start | bytes 98312 | tf_op jit(solution)/shard_map/ppermute | solution.py:18
  169.2 7.5 %collective-permute-start.18 = (f32[64,48,1]{0,1,2:T(8,128)S(1)}, f32[64,48,1]{0,1,2:T(8,128)S(1)}, u32[]{:S(2)}, u32[]{:S(2)}) collective-permute-start(f32[64,48,1]{0,1,2:T(8,128)S(1)} %copy.49), channel_id=1, source_target_pairs={{0,1},{1,2},{2,3},{3,4},{4,5},{5,6},{6,7},{7,8},{8,9},{9,10},{10,1... | collective-permute-start | bytes 36872 | tf_op jit(solution)/shard_map/ppermute | solution.py:17
  176.8 2.8 fusion.106
  184.9 9.0 %fusion.81 = (f32[64,48,128]{2,0,1:T(8,128)S(1)}, f32[64,48,128]{2,0,1:T(8,128)}) fusion(f32[64,48,128]{2,0,1:T(8,128)S(1)} %fusion.13, f32[48,128,64]{1,2,0:T(8,128)S(1)} %copy-done.23, f32[64]{0:T(128)S(1)} %copy-done.38, f32[48,128]{1,0:T(8,128)S(1)} %convert_element_type.25, f32[48,128]{1,0:T(8,128)S(1)} %subtract_convert_fusion, ...), kind=kOutput, calls=%fused_computation.163 | convolution fusion | flops 319684608 | bytes 9593088 | tf_op jit(solution)/shard_map/dc,chw->dhw/dot_general | solution.py:30
  195.9 4.1 %collective-permute-start.21 = (f32[64,1,128]{2,0,1:T(8,128)S(1)}, f32[64,1,128]{2,0,1:T(8,128)S(1)}, u32[]{:S(2)}, u32[]{:S(2)}) collective-permute-start(f32[64,1,128]{2,0,1:T(8,128)S(1)} %get-tuple-element.16), channel_id=1, source_target_pairs={{16,0},{32,16},{48,32},{64,48},{80,64},{96,80},{112,96},{17,1},{33... | collective-permute-start | bytes 98312 | tf_op jit(solution)/shard_map/ppermute | solution.py:18
  204.3 6.5 %collective-permute-start.22 = (f32[64,48,1]{0,1,2:T(8,128)S(1)}, f32[64,48,1]{0,1,2:T(8,128)S(1)}, u32[]{:S(2)}, u32[]{:S(2)}) collective-permute-start(f32[64,48,1]{0,1,2:T(8,128)S(1)} %copy.53), channel_id=1, source_target_pairs={{0,1},{1,2},{2,3},{3,4},{4,5},{5,6},{6,7},{7,8},{8,9},{9,10},{10,1... | collective-permute-start | bytes 36872 | tf_op jit(solution)/shard_map/ppermute | solution.py:17
  216.8 4.6 %collective-permute-done.23 = f32[64,48,1]{0,1,2:T(8,128)S(1)} collective-permute-done((f32[64,48,1]{0,1,2:T(8,128)S(1)}, f32[64,48,1]{0,1,2:T(8,128)S(1)}, u32[]{:S(2)}, u32[]{:S(2)}) %collective-permute-start.23) | collective-permute-done | bytes 12320 | tf_op jit(solution)/shard_map/ppermute | solution.py:18
  227.6 7.6 %fusion.20 = f32[64,48,128]{2,0,1:T(8,128)S(1)} fusion(f32[64,48,128]{2,0,1:T(8,128)S(1)} %fusion.13, f32[48,128,64]{1,2,0:T(8,128)S(1)} %fusion.183, f32[48,128,64]{1,2,0:T(8,128)S(1)} %fusion.127, f32[64,48,128]{2,0,1:T(8,128)S(1)} %copy-done.42, f32[48,128,64]{1,2,0:T(8,128)S(1)} %copy-done.24, f32[48,128,64]{1,2,0:T(8,128)S(1)} %copy-done.14, ...), kind=kOutput, calls=%fused_computation.28 | convolution fusion | flops 316538880 | bytes 12738816 | tf_op jit(solution)/shard_map/dc,chw->dhw/dot_general | solution.py:30
  239.0 4.3 %collective-permute-start.25 = (f32[64,1,128]{2,0,1:T(8,128)S(1)}, f32[64,1,128]{2,0,1:T(8,128)S(1)}, u32[]{:S(2)}, u32[]{:S(2)}) collective-permute-start(f32[64,1,128]{2,0,1:T(8,128)S(1)} %get-tuple-element.12), channel_id=1, source_target_pairs={{16,0},{32,16},{48,32},{64,48},{80,64},{96,80},{112,96},{17,1},{33... | collective-permute-start | bytes 98312 | tf_op jit(solution)/shard_map/ppermute | solution.py:18
  247.6 7.4 %collective-permute-start.26 = (f32[64,48,1]{0,1,2:T(8,128)S(1)}, f32[64,48,1]{0,1,2:T(8,128)S(1)}, u32[]{:S(2)}, u32[]{:S(2)}) collective-permute-start(f32[64,48,1]{0,1,2:T(8,128)S(1)} %copy.57), channel_id=1, source_target_pairs={{0,1},{1,2},{2,3},{3,4},{4,5},{5,6},{6,7},{7,8},{8,9},{9,10},{10,1... | collective-permute-start | bytes 36872 | tf_op jit(solution)/shard_map/ppermute | solution.py:17
  263.2 9.0 %fusion.76 = (f32[64,48,128]{2,0,1:T(8,128)S(1)}, f32[64,48,128]{2,0,1:T(8,128)}) fusion(f32[64,48,128]{2,0,1:T(8,128)S(1)} %fusion.20, f32[48,128,64]{1,2,0:T(8,128)S(1)} %copy-done.19, f32[64]{0:T(128)S(1)} %copy-done.38, f32[48,128]{1,0:T(8,128)S(1)} %convert_element_type.25, f32[48,128]{1,0:T(8,128)S(1)} %subtract_convert_fusion, ...), kind=kOutput, calls=%fused_computation.152 | convolution fusion | flops 319684608 | bytes 9593088 | tf_op jit(solution)/shard_map/dc,chw->dhw/dot_general | solution.py:30
  274.1 4.2 %collective-permute-start.29 = (f32[64,1,128]{2,0,1:T(8,128)S(1)}, f32[64,1,128]{2,0,1:T(8,128)S(1)}, u32[]{:S(2)}, u32[]{:S(2)}) collective-permute-start(f32[64,1,128]{2,0,1:T(8,128)S(1)} %get-tuple-element.8), channel_id=1, source_target_pairs={{16,0},{32,16},{48,32},{64,48},{80,64},{96,80},{112,96},{17,1},{33... | collective-permute-start | bytes 98312 | tf_op jit(solution)/shard_map/ppermute | solution.py:18
  282.5 6.3 %collective-permute-start.30 = (f32[64,48,1]{0,1,2:T(8,128)S(1)}, f32[64,48,1]{0,1,2:T(8,128)S(1)}, u32[]{:S(2)}, u32[]{:S(2)}) collective-permute-start(f32[64,48,1]{0,1,2:T(8,128)S(1)} %copy.61), channel_id=1, source_target_pairs={{0,1},{1,2},{2,3},{3,4},{4,5},{5,6},{6,7},{7,8},{8,9},{9,10},{10,1... | collective-permute-start | bytes 36872 | tf_op jit(solution)/shard_map/ppermute | solution.py:17
  294.6 4.9 %collective-permute-done.31 = f32[64,48,1]{0,1,2:T(8,128)S(1)} collective-permute-done((f32[64,48,1]{0,1,2:T(8,128)S(1)}, f32[64,48,1]{0,1,2:T(8,128)S(1)}, u32[]{:S(2)}, u32[]{:S(2)}) %collective-permute-start.31) | collective-permute-done | bytes 12320 | tf_op jit(solution)/shard_map/ppermute | solution.py:18
  305.8 3.9 %fusion.27 = f32[64,48,128]{2,0,1:T(8,128)S(1)} fusion(f32[64,48,128]{2,0,1:T(8,128)S(1)} %fusion.20, f32[48,128,64]{1,2,0:T(8,128)S(1)} %fusion.180, f32[48,128,64]{1,2,0:T(8,128)S(1)} %fusion.122, f32[64,48,128]{2,0,1:T(8,128)S(1)} %copy-done.40, f32[48,128,64]{1,2,0:T(8,128)S(1)} %copy-done.20, f32[48,128,64]{1,2,0:T(8,128)S(1)} %copy-done.16, ...), kind=kOutput, calls=%fused_computation.35 | convolution fusion | flops 316538880 | bytes 12738816 | tf_op jit(solution)/shard_map/dc,chw->dhw/dot_general | solution.py:30
  (199 shorter events, 138.2 us)
Async XLA Ops:
  2.1 30.7 %collective-permute-start = (f32[64,1,128]{2,0,1:T(8,128)S(1)}, f32[64,1,128]{2,0,1:T(8,128)S(1)}, u32[]{:S(2)}, u32[]{:S(2)}) collective-permute-start(f32[64,1,128]{2,0,1:T(8,128)S(1)} %get-tuple-element.35), channel_id=1, source_target_pairs={{0,16},{16,32},{32,48},{48,64},{64,80},{80,96},{96,112},{1,17},{17... | collective-permute-start | bytes 98312 | tf_op jit(solution)/shard_map/ppermute | solution.py:17
  5.6 27.6 %collective-permute-start.1 = (f32[64,1,128]{2,0,1:T(8,128)S(1)}, f32[64,1,128]{2,0,1:T(8,128)S(1)}, u32[]{:S(2)}, u32[]{:S(2)}) collective-permute-start(f32[64,1,128]{2,0,1:T(8,128)S(1)} %get-tuple-element.36), channel_id=1, source_target_pairs={{16,0},{32,16},{48,32},{64,48},{80,64},{96,80},{112,96},{17,1},{33... | collective-permute-start | bytes 98312 | tf_op jit(solution)/shard_map/ppermute | solution.py:18
  12.4 18.6 %collective-permute-start.3 = (f32[64,48,1]{0,1,2:T(8,128)S(1)}, f32[64,48,1]{0,1,2:T(8,128)S(1)}, u32[]{:S(2)}, u32[]{:S(2)}) collective-permute-start(f32[64,48,1]{0,1,2:T(8,128)S(1)} %copy.67), channel_id=1, source_target_pairs={{1,0},{2,1},{3,2},{4,3},{5,4},{6,5},{7,6},{8,7},{9,8},{10,9},{11,1... | collective-permute-start | bytes 36872 | tf_op jit(solution)/shard_map/ppermute | solution.py:18
  17.6 11.7 %collective-permute-start.2 = (f32[64,48,1]{0,1,2:T(8,128)S(1)}, f32[64,48,1]{0,1,2:T(8,128)S(1)}, u32[]{:S(2)}, u32[]{:S(2)}) collective-permute-start(f32[64,48,1]{0,1,2:T(8,128)S(1)} %copy.66), channel_id=1, source_target_pairs={{0,1},{1,2},{2,3},{3,4},{4,5},{5,6},{6,7},{7,8},{8,9},{9,10},{10,1... | collective-permute-start | bytes 36872 | tf_op jit(solution)/shard_map/ppermute | solution.py:17
  44.0 26.5 %collective-permute-start.4 = (f32[64,1,128]{2,0,1:T(8,128)S(1)}, f32[64,1,128]{2,0,1:T(8,128)S(1)}, u32[]{:S(2)}, u32[]{:S(2)}) collective-permute-start(f32[64,1,128]{2,0,1:T(8,128)S(1)} %get-tuple-element.31), channel_id=1, source_target_pairs={{0,16},{16,32},{32,48},{48,64},{64,80},{80,96},{96,112},{1,17},{17... | collective-permute-start | bytes 98312 | tf_op jit(solution)/shard_map/ppermute | solution.py:17
  46.6 23.9 %collective-permute-start.5 = (f32[64,1,128]{2,0,1:T(8,128)S(1)}, f32[64,1,128]{2,0,1:T(8,128)S(1)}, u32[]{:S(2)}, u32[]{:S(2)}) collective-permute-start(f32[64,1,128]{2,0,1:T(8,128)S(1)} %get-tuple-element.32), channel_id=1, source_target_pairs={{16,0},{32,16},{48,32},{64,48},{80,64},{96,80},{112,96},{17,1},{33... | collective-permute-start | bytes 98312 | tf_op jit(solution)/shard_map/ppermute | solution.py:18
  54.3 8.1 %collective-permute-start.6 = (f32[64,48,1]{0,1,2:T(8,128)S(1)}, f32[64,48,1]{0,1,2:T(8,128)S(1)}, u32[]{:S(2)}, u32[]{:S(2)}) collective-permute-start(f32[64,48,1]{0,1,2:T(8,128)S(1)} %copy.36), channel_id=1, source_target_pairs={{0,1},{1,2},{2,3},{3,4},{4,5},{5,6},{6,7},{7,8},{8,9},{9,10},{10,1... | collective-permute-start | bytes 36872 | tf_op jit(solution)/shard_map/ppermute | solution.py:17
  60.0 8.8 %collective-permute-start.7 = (f32[64,48,1]{0,1,2:T(8,128)S(1)}, f32[64,48,1]{0,1,2:T(8,128)S(1)}, u32[]{:S(2)}, u32[]{:S(2)}) collective-permute-start(f32[64,48,1]{0,1,2:T(8,128)S(1)} %copy.38), channel_id=1, source_target_pairs={{1,0},{2,1},{3,2},{4,3},{5,4},{6,5},{7,6},{8,7},{9,8},{10,9},{11,1... | collective-permute-start | bytes 36872 | tf_op jit(solution)/shard_map/ppermute | solution.py:18
  80.4 24.4 %collective-permute-start.8 = (f32[64,1,128]{2,0,1:T(8,128)S(1)}, f32[64,1,128]{2,0,1:T(8,128)S(1)}, u32[]{:S(2)}, u32[]{:S(2)}) collective-permute-start(f32[64,1,128]{2,0,1:T(8,128)S(1)} %get-tuple-element.27), channel_id=1, source_target_pairs={{0,16},{16,32},{32,48},{48,64},{64,80},{80,96},{96,112},{1,17},{17... | collective-permute-start | bytes 98312 | tf_op jit(solution)/shard_map/ppermute | solution.py:17
  82.3 22.5 %collective-permute-start.9 = (f32[64,1,128]{2,0,1:T(8,128)S(1)}, f32[64,1,128]{2,0,1:T(8,128)S(1)}, u32[]{:S(2)}, u32[]{:S(2)}) collective-permute-start(f32[64,1,128]{2,0,1:T(8,128)S(1)} %get-tuple-element.28), channel_id=1, source_target_pairs={{16,0},{32,16},{48,32},{64,48},{80,64},{96,80},{112,96},{17,1},{33... | collective-permute-start | bytes 98312 | tf_op jit(solution)/shard_map/ppermute | solution.py:18
  89.1 13.9 %collective-permute-start.11 = (f32[64,48,1]{0,1,2:T(8,128)S(1)}, f32[64,48,1]{0,1,2:T(8,128)S(1)}, u32[]{:S(2)}, u32[]{:S(2)}) collective-permute-start(f32[64,48,1]{0,1,2:T(8,128)S(1)} %copy.43), channel_id=1, source_target_pairs={{1,0},{2,1},{3,2},{4,3},{5,4},{6,5},{7,6},{8,7},{9,8},{10,9},{11,1... | collective-permute-start | bytes 36872 | tf_op jit(solution)/shard_map/ppermute | solution.py:18
  91.1 10.3 %collective-permute-start.10 = (f32[64,48,1]{0,1,2:T(8,128)S(1)}, f32[64,48,1]{0,1,2:T(8,128)S(1)}, u32[]{:S(2)}, u32[]{:S(2)}) collective-permute-start(f32[64,48,1]{0,1,2:T(8,128)S(1)} %copy.41), channel_id=1, source_target_pairs={{0,1},{1,2},{2,3},{3,4},{4,5},{5,6},{6,7},{7,8},{8,9},{9,10},{10,1... | collective-permute-start | bytes 36872 | tf_op jit(solution)/shard_map/ppermute | solution.py:17
  115.6 29.1 %collective-permute-start.12 = (f32[64,1,128]{2,0,1:T(8,128)S(1)}, f32[64,1,128]{2,0,1:T(8,128)S(1)}, u32[]{:S(2)}, u32[]{:S(2)}) collective-permute-start(f32[64,1,128]{2,0,1:T(8,128)S(1)} %get-tuple-element.23), channel_id=1, source_target_pairs={{0,16},{16,32},{32,48},{48,64},{64,80},{80,96},{96,112},{1,17},{17... | collective-permute-start | bytes 98312 | tf_op jit(solution)/shard_map/ppermute | solution.py:17
  117.7 27.0 %collective-permute-start.13 = (f32[64,1,128]{2,0,1:T(8,128)S(1)}, f32[64,1,128]{2,0,1:T(8,128)S(1)}, u32[]{:S(2)}, u32[]{:S(2)}) collective-permute-start(f32[64,1,128]{2,0,1:T(8,128)S(1)} %get-tuple-element.24), channel_id=1, source_target_pairs={{16,0},{32,16},{48,32},{64,48},{80,64},{96,80},{112,96},{17,1},{33... | collective-permute-start | bytes 98312 | tf_op jit(solution)/shard_map/ppermute | solution.py:18
  126.0 10.4 %collective-permute-start.14 = (f32[64,48,1]{0,1,2:T(8,128)S(1)}, f32[64,48,1]{0,1,2:T(8,128)S(1)}, u32[]{:S(2)}, u32[]{:S(2)}) collective-permute-start(f32[64,48,1]{0,1,2:T(8,128)S(1)} %copy.45), channel_id=1, source_target_pairs={{0,1},{1,2},{2,3},{3,4},{4,5},{5,6},{6,7},{7,8},{8,9},{9,10},{10,1... | collective-permute-start | bytes 36872 | tf_op jit(solution)/shard_map/ppermute | solution.py:17
  134.2 8.8 %collective-permute-start.15 = (f32[64,48,1]{0,1,2:T(8,128)S(1)}, f32[64,48,1]{0,1,2:T(8,128)S(1)}, u32[]{:S(2)}, u32[]{:S(2)}) collective-permute-start(f32[64,48,1]{0,1,2:T(8,128)S(1)} %copy.47), channel_id=1, source_target_pairs={{1,0},{2,1},{3,2},{4,3},{5,4},{6,5},{7,6},{8,7},{9,8},{10,9},{11,1... | collective-permute-start | bytes 36872 | tf_op jit(solution)/shard_map/ppermute | solution.py:18
  158.7 24.4 %collective-permute-start.16 = (f32[64,1,128]{2,0,1:T(8,128)S(1)}, f32[64,1,128]{2,0,1:T(8,128)S(1)}, u32[]{:S(2)}, u32[]{:S(2)}) collective-permute-start(f32[64,1,128]{2,0,1:T(8,128)S(1)} %get-tuple-element.19), channel_id=1, source_target_pairs={{0,16},{16,32},{32,48},{48,64},{64,80},{80,96},{96,112},{1,17},{17... | collective-permute-start | bytes 98312 | tf_op jit(solution)/shard_map/ppermute | solution.py:17
  160.6 22.5 %collective-permute-start.17 = (f32[64,1,128]{2,0,1:T(8,128)S(1)}, f32[64,1,128]{2,0,1:T(8,128)S(1)}, u32[]{:S(2)}, u32[]{:S(2)}) collective-permute-start(f32[64,1,128]{2,0,1:T(8,128)S(1)} %get-tuple-element.20), channel_id=1, source_target_pairs={{16,0},{32,16},{48,32},{64,48},{80,64},{96,80},{112,96},{17,1},{33... | collective-permute-start | bytes 98312 | tf_op jit(solution)/shard_map/ppermute | solution.py:18
  167.3 14.0 %collective-permute-start.19 = (f32[64,48,1]{0,1,2:T(8,128)S(1)}, f32[64,48,1]{0,1,2:T(8,128)S(1)}, u32[]{:S(2)}, u32[]{:S(2)}) collective-permute-start(f32[64,48,1]{0,1,2:T(8,128)S(1)} %copy.51), channel_id=1, source_target_pairs={{1,0},{2,1},{3,2},{4,3},{5,4},{6,5},{7,6},{8,7},{9,8},{10,9},{11,1... | collective-permute-start | bytes 36872 | tf_op jit(solution)/shard_map/ppermute | solution.py:18
  169.2 10.4 %collective-permute-start.18 = (f32[64,48,1]{0,1,2:T(8,128)S(1)}, f32[64,48,1]{0,1,2:T(8,128)S(1)}, u32[]{:S(2)}, u32[]{:S(2)}) collective-permute-start(f32[64,48,1]{0,1,2:T(8,128)S(1)} %copy.49), channel_id=1, source_target_pairs={{0,1},{1,2},{2,3},{3,4},{4,5},{5,6},{6,7},{7,8},{8,9},{9,10},{10,1... | collective-permute-start | bytes 36872 | tf_op jit(solution)/shard_map/ppermute | solution.py:17
  193.9 29.2 %collective-permute-start.20 = (f32[64,1,128]{2,0,1:T(8,128)S(1)}, f32[64,1,128]{2,0,1:T(8,128)S(1)}, u32[]{:S(2)}, u32[]{:S(2)}) collective-permute-start(f32[64,1,128]{2,0,1:T(8,128)S(1)} %get-tuple-element.15), channel_id=1, source_target_pairs={{0,16},{16,32},{32,48},{48,64},{64,80},{80,96},{96,112},{1,17},{17... | collective-permute-start | bytes 98312 | tf_op jit(solution)/shard_map/ppermute | solution.py:17
  195.9 27.2 %collective-permute-start.21 = (f32[64,1,128]{2,0,1:T(8,128)S(1)}, f32[64,1,128]{2,0,1:T(8,128)S(1)}, u32[]{:S(2)}, u32[]{:S(2)}) collective-permute-start(f32[64,1,128]{2,0,1:T(8,128)S(1)} %get-tuple-element.16), channel_id=1, source_target_pairs={{16,0},{32,16},{48,32},{64,48},{80,64},{96,80},{112,96},{17,1},{33... | collective-permute-start | bytes 98312 | tf_op jit(solution)/shard_map/ppermute | solution.py:18
  204.3 10.8 %collective-permute-start.22 = (f32[64,48,1]{0,1,2:T(8,128)S(1)}, f32[64,48,1]{0,1,2:T(8,128)S(1)}, u32[]{:S(2)}, u32[]{:S(2)}) collective-permute-start(f32[64,48,1]{0,1,2:T(8,128)S(1)} %copy.53), channel_id=1, source_target_pairs={{0,1},{1,2},{2,3},{3,4},{4,5},{5,6},{6,7},{7,8},{8,9},{9,10},{10,1... | collective-permute-start | bytes 36872 | tf_op jit(solution)/shard_map/ppermute | solution.py:17
  212.7 8.8 %collective-permute-start.23 = (f32[64,48,1]{0,1,2:T(8,128)S(1)}, f32[64,48,1]{0,1,2:T(8,128)S(1)}, u32[]{:S(2)}, u32[]{:S(2)}) collective-permute-start(f32[64,48,1]{0,1,2:T(8,128)S(1)} %copy.55), channel_id=1, source_target_pairs={{1,0},{2,1},{3,2},{4,3},{5,4},{6,5},{7,6},{8,7},{9,8},{10,9},{11,1... | collective-permute-start | bytes 36872 | tf_op jit(solution)/shard_map/ppermute | solution.py:18
  237.1 24.3 %collective-permute-start.24 = (f32[64,1,128]{2,0,1:T(8,128)S(1)}, f32[64,1,128]{2,0,1:T(8,128)S(1)}, u32[]{:S(2)}, u32[]{:S(2)}) collective-permute-start(f32[64,1,128]{2,0,1:T(8,128)S(1)} %get-tuple-element.11), channel_id=1, source_target_pairs={{0,16},{16,32},{32,48},{48,64},{64,80},{80,96},{96,112},{1,17},{17... | collective-permute-start | bytes 98312 | tf_op jit(solution)/shard_map/ppermute | solution.py:17
  239.0 22.4 %collective-permute-start.25 = (f32[64,1,128]{2,0,1:T(8,128)S(1)}, f32[64,1,128]{2,0,1:T(8,128)S(1)}, u32[]{:S(2)}, u32[]{:S(2)}) collective-permute-start(f32[64,1,128]{2,0,1:T(8,128)S(1)} %get-tuple-element.12), channel_id=1, source_target_pairs={{16,0},{32,16},{48,32},{64,48},{80,64},{96,80},{112,96},{17,1},{33... | collective-permute-start | bytes 98312 | tf_op jit(solution)/shard_map/ppermute | solution.py:18
  245.7 13.9 %collective-permute-start.27 = (f32[64,48,1]{0,1,2:T(8,128)S(1)}, f32[64,48,1]{0,1,2:T(8,128)S(1)}, u32[]{:S(2)}, u32[]{:S(2)}) collective-permute-start(f32[64,48,1]{0,1,2:T(8,128)S(1)} %copy.59), channel_id=1, source_target_pairs={{1,0},{2,1},{3,2},{4,3},{5,4},{6,5},{7,6},{8,7},{9,8},{10,9},{11,1... | collective-permute-start | bytes 36872 | tf_op jit(solution)/shard_map/ppermute | solution.py:18
  247.6 10.3 %collective-permute-start.26 = (f32[64,48,1]{0,1,2:T(8,128)S(1)}, f32[64,48,1]{0,1,2:T(8,128)S(1)}, u32[]{:S(2)}, u32[]{:S(2)}) collective-permute-start(f32[64,48,1]{0,1,2:T(8,128)S(1)} %copy.57), channel_id=1, source_target_pairs={{0,1},{1,2},{2,3},{3,4},{4,5},{5,6},{6,7},{7,8},{8,9},{9,10},{10,1... | collective-permute-start | bytes 36872 | tf_op jit(solution)/shard_map/ppermute | solution.py:17
  272.2 29.1 %collective-permute-start.28 = (f32[64,1,128]{2,0,1:T(8,128)S(1)}, f32[64,1,128]{2,0,1:T(8,128)S(1)}, u32[]{:S(2)}, u32[]{:S(2)}) collective-permute-start(f32[64,1,128]{2,0,1:T(8,128)S(1)} %get-tuple-element.7), channel_id=1, source_target_pairs={{0,16},{16,32},{32,48},{48,64},{64,80},{80,96},{96,112},{1,17},{17... | collective-permute-start | bytes 98312 | tf_op jit(solution)/shard_map/ppermute | solution.py:17
  274.1 27.1 %collective-permute-start.29 = (f32[64,1,128]{2,0,1:T(8,128)S(1)}, f32[64,1,128]{2,0,1:T(8,128)S(1)}, u32[]{:S(2)}, u32[]{:S(2)}) collective-permute-start(f32[64,1,128]{2,0,1:T(8,128)S(1)} %get-tuple-element.8), channel_id=1, source_target_pairs={{16,0},{32,16},{48,32},{64,48},{80,64},{96,80},{112,96},{17,1},{33... | collective-permute-start | bytes 98312 | tf_op jit(solution)/shard_map/ppermute | solution.py:18
  282.5 10.4 %collective-permute-start.30 = (f32[64,48,1]{0,1,2:T(8,128)S(1)}, f32[64,48,1]{0,1,2:T(8,128)S(1)}, u32[]{:S(2)}, u32[]{:S(2)}) collective-permute-start(f32[64,48,1]{0,1,2:T(8,128)S(1)} %copy.61), channel_id=1, source_target_pairs={{0,1},{1,2},{2,3},{3,4},{4,5},{5,6},{6,7},{7,8},{8,9},{9,10},{10,1... | collective-permute-start | bytes 36872 | tf_op jit(solution)/shard_map/ppermute | solution.py:17
  290.8 8.8 %collective-permute-start.31 = (f32[64,48,1]{0,1,2:T(8,128)S(1)}, f32[64,48,1]{0,1,2:T(8,128)S(1)}, u32[]{:S(2)}, u32[]{:S(2)}) collective-permute-start(f32[64,48,1]{0,1,2:T(8,128)S(1)} %copy.63), channel_id=1, source_target_pairs={{1,0},{2,1},{3,2},{4,3},{5,4},{6,5},{7,6},{8,7},{9,8},{10,9},{11,1... | collective-permute-start | bytes 36872 | tf_op jit(solution)/shard_map/ppermute | solution.py:18
  (43 other events, 239.4 us)
where the time goes:
time: 316 us; the launch traced here: 312 us
  starting transfers between devices  119 us (38%)
  matrix products  95.6 us (30%)
  local copies, waits for them, and re-layouts  77.2 us (24%)
  waiting for transfers between devices  19 us (6%)
    dot_general x24, matrix products, mixing(): jnp.einsum('dc,chw->dhw', matrix, values, precision=lax.Precision.HIGHEST)  93.7 us
    ppermute x16, starting transfers between devices, with_halo(): lax.ppermute(last, axis, up)  69.5 us
    ppermute x16, starting transfers between devices, with_halo(): lax.ppermute(leading, axis, [(b, a) for a, b in up])  49.5 us
    slice x23, local copies, waits for them, and re-layouts, with_halo(): last = lax.slice_in_dim(x, length - width, length, axis=dim)  29.9 us
    ppermute x16, waiting for transfers between devices, with_halo(): lax.ppermute(leading, axis, [(b, a) for a, b in up])  18.9 us
    ppermute x8, local copies, waits for them, and re-layouts, with_halo(): lax.ppermute(last, axis, up)  13.8 us
    ppermute x8, local copies, waits for them, and re-layouts, with_halo(): lax.ppermute(leading, axis, [(b, a) for a, b in up])  13.7 us
    slice x7, local copies, waits for them, and re-layouts, with_halo(): leading = lax.slice_in_dim(x, 0, width, axis=dim)  9.29 us
  transfers between devices with their start and end apart: 32, of which 4 were waited for; matrix products, arithmetic and copies ran while one was open for 26% of the time, Pallas kernels for 0%

commit v1 on v0

v1 whole, which is shorter than its diff:
```python
import jax
import jax.numpy as jnp
from jax import lax
from jax.experimental import pallas as pl
from jax.experimental.pallas import tpu as pltpu
from jax.sharding import PartitionSpec as P

ITERS = 4
HALO = 2 * ITERS
C, ROWS, COLS = 64, 48, 128
HALF = ROWS + 2 * HALO
TILES = COLS // 2 + HALO
PLANES = C + 8
GROUP = 24
BF = jnp.bfloat16
F32 = jnp.float32


def split(x):
    hi = x.astype(BF)
    return hi, (x - hi.astype(F32)).astype(BF)


def mirror(x):
    lane = lax.broadcasted_iota(jnp.int32, x.shape, 1)
    idx = jnp.where(lane < 64, lane, 191 - lane)
    return jnp.take_along_axis(x, idx, axis=1)


def turn_kernel(x_ref, m_ref, top_ref, bot_ref, out_ref, left_ref, right_ref):
    flat = out_ref.reshape(64 * PLANES, 128)

    def plane(ch, rows):
        p = jnp.concatenate([top_ref[ch], rows, bot_ref[ch]], axis=0)
        q = mirror(p)
        stacked = jnp.concatenate([q, pltpu.roll(q, 64, 1)], axis=0)
        flat[pl.ds(ch, 64, stride=PLANES), :] = stacked.T[0:64, :]

    def loop(i, _):
        for k in range(8):
            plane(i * 8 + k, x_ref[i * 8 + k])
        return 0

    lax.fori_loop(0, C // 8, loop, 0)
    for k in range(3):
        plane(C + k, m_ref[k])
    for j in range(64):
        out_ref[j, C + 3 :, :] = jnp.zeros((5, 128), F32)
    low = lax.broadcasted_iota(jnp.int32, (PLANES, 128), 1) < 64
    for t in range(4):
        near, far = out_ref[t], pltpu.roll(out_ref[4 + t], 64, 1)
        left_ref[t] = jnp.where(low, near, far)
        right_ref[t] = jnp.where(low, far, near)


def turn(x, masks, top, bot):
    message = jax.ShapeDtypeStruct((4, PLANES, 128), F32)
    return pl.pallas_call(
        turn_kernel,
        name="turn",
        out_shape=(jax.ShapeDtypeStruct((64, PLANES, 128), F32), message, message),
        compiler_params=pltpu.CompilerParams(vmem_limit_bytes=48 * 2**20),
    )(x, masks, top, bot)


def stages_kernel(
    f_ref, left_ref, right_ref, rate_ref, heat_ref, rows_ref, cols_ref, react_ref,
    out_ref, A, B, brate, burn, lit, w_mix, w_react, table,
):
    r_hi, r_lo = split(rows_ref[...])
    c_hi, c_lo = split(cols_ref[...])
    e_hi, e_lo = split(react_ref[...])
    zero = jnp.zeros((64, 64), BF)
    w_mix[0:64, :] = jnp.concatenate([r_hi, c_hi, r_hi, c_hi], 1)
    w_mix[64:128, :] = jnp.concatenate([r_lo, c_lo, zero, zero], 1)
    table[...] = jnp.zeros_like(table)
    table[0:13, 0:64] = rate_ref[...]
    table[13:14, 0:64] = heat_ref[...]
    by_channel = table[...].T[0:64, :]
    t_hi, t_lo = split(by_channel)
    h_hi, h_lo = split(by_channel[:, 13:14])
    lane = lax.broadcasted_iota(jnp.int32, (64, 64), 1)
    heat = jnp.where(lane == 0, h_hi.astype(F32), jnp.where(lane == 1, h_lo.astype(F32), 0.0))
    w_react[...] = jnp.concatenate([e_hi, e_hi, e_lo, heat.astype(BF)], 1)
    w_rate = jnp.concatenate([t_hi, t_lo], 1)

    low = lax.broadcasted_iota(jnp.int32, (PLANES, 128), 1) < 64
    classes = lax.broadcasted_iota(jnp.int32, (128, 128), 0).astype(F32)

    def place(j, tile):
        A[j + 1] = tile[0:C]
        m = tile[C : C + 8]
        burn[j] = jnp.broadcast_to(m[1:2], (8, 128))
        onehot = jnp.where(classes == m[0:1], m[1:2], 0.0).astype(BF)
        brate[j] = jnp.dot(w_rate, jnp.concatenate([onehot, onehot], 0), preferred_element_type=F32)
        lit[j] = jnp.where(classes[0:16] < 2, m[2:3], 0.0).astype(BF)

    for t in range(4):
        from_right, from_left = left_ref[t], right_ref[t]
        place(7 - t, pltpu.roll(jnp.where(low, from_right, from_left), 64, 1))
        place(3 - t, jnp.where(low, from_left, from_right))

    def fill(i, _):
        for k in range(16):
            place(HALO + i * 16 + k, f_ref[i * 16 + k])
        return 0

    lax.fori_loop(0, 4, fill, 0)
    A[0] = jnp.zeros((C, 128), F32)
    B[0] = jnp.zeros((C, 128), F32)
    A[TILES + 1] = pltpu.roll(A[TILES], 64, 1)

    def block(src, dst, b, second):
        xs = [src[b + k] for k in range(GROUP + 2)]
        for p in range(0, GROUP, 2):
            plain, mix, react = [], [], []
            for k in (p, p + 1):
                x = xs[k + 1]
                x2 = x + x
                v = pltpu.roll(x, 1, 1) + pltpu.roll(x, 127, 1) - x2
                h = xs[k] + xs[k + 2] - x2
                v_hi, v_lo = split(v)
                h_hi, h_lo = split(h)
                s_hi, s_lo = split(jnp.tanh(x))
                mix.append(jnp.concatenate([v_hi, h_hi, v_lo, h_lo], 0))
                react.append(jnp.concatenate([s_hi, s_lo, s_hi, lit[b + k], jnp.zeros((48, 128), BF)], 0))
                plain.append(v + h)
            mm = jnp.dot(w_mix[...], jnp.concatenate(mix, 1), preferred_element_type=F32)
            rr = jnp.dot(w_react[...], jnp.concatenate(react, 1), preferred_element_type=F32)
            for i, k in enumerate((p, p + 1)):
                at = slice(128 * i, 128 * i + 128)
                mixed = plain[i] + (mm[0:64, at] + mm[64:128, at])
                drive = brate[b + k] * mixed + burn[b + k][0:1] * rr[:, at]
                if not second:
                    dst[b + k + 1] = 0.5 * xs[k + 1] + drive
                else:
                    dst[b + k + 1] = 0.5 * dst[b + k + 1] + (0.25 * xs[k + 1] + 0.5 * drive)

    def step(s, _):
        def first(i, _):
            block(A, B, i * GROUP, False)
            return 0

        def second(i, _):
            block(B, A, i * GROUP, True)
            return 0

        lax.fori_loop((2 * s + 1) // GROUP, TILES // GROUP, first, 0)
        B[TILES + 1] = pltpu.roll(B[TILES], 64, 1)
        lax.fori_loop((2 * s + 2) // GROUP, TILES // GROUP, second, 0)
        A[TILES + 1] = pltpu.roll(A[TILES], 64, 1)
        return 0

    lax.fori_loop(0, ITERS, step, 0)

    flat = A.reshape((TILES + 2) * C, 128)
    is_low = lax.broadcasted_iota(jnp.int32, (ROWS, 128), 1) < 64

    def back(i, _):
        for k in range(8):
            ch = i * 8 + k
            tiles = flat[pl.ds((HALO + 1) * C + ch, 64, stride=C), :]
            turned = tiles.T
            both = jnp.concatenate([turned[HALO : HALO + ROWS], turned[64 + HALO : 64 + HALO + ROWS]], 1)
            out_ref[ch] = mirror(both)
        return 0

    lax.fori_loop(0, C // 8, back, 0)


def stages(field, left, right, *params):
    return pl.pallas_call(
        stages_kernel,
        name="stages",
        out_shape=jax.ShapeDtypeStruct((C, ROWS, COLS), F32),
        scratch_shapes=[
            pltpu.VMEM((TILES + 2, C, 128), F32),
            pltpu.VMEM((TILES + 2, C, 128), F32),
            pltpu.VMEM((TILES, C, 128), F32),
            pltpu.VMEM((TILES, 8, 128), F32),
            pltpu.VMEM((TILES, 16, 128), BF),
            pltpu.VMEM((128, 256), BF),
            pltpu.VMEM((64, 256), BF),
            pltpu.VMEM((128, 128), F32),
        ],
        compiler_params=pltpu.CompilerParams(vmem_limit_bytes=56 * 2**20),
    )(field, left, right, *params)


def exchange(to_lower, to_upper, axis):
    up = [(i, i + 1) for i in range(lax.axis_size(axis) - 1)]
    down = [(b, a) for a, b in up]
    return lax.ppermute(to_lower, axis, down), lax.ppermute(to_upper, axis, up)


def per_device(
    fire_state, fuel_class, firebreak, ignition,
    spread_rate, spread_rows, spread_cols, reaction, ignition_heat,
):
    masks = jnp.stack([fuel_class, 1 - firebreak, ignition]).astype(F32)
    first = jnp.concatenate([fire_state[:, :HALO], masks[:, :HALO]], 0)
    last = jnp.concatenate([fire_state[:, ROWS - HALO :], masks[:, ROWS - HALO :]], 0)
    bot, top = exchange(first, last, "row")
    field, left, right = turn(fire_state, masks, top, bot)
    from_right, from_left = exchange(left, right, "col")
    return stages(
        field, from_right, from_left,
        spread_rate, ignition_heat[None], spread_rows, spread_cols, reaction,
    )


def solution(mesh):
    whole = P(None, "row", "col")
    cells = P("row", "col")
    return jax.shard_map(
        per_device,
        mesh=mesh,
        in_specs=(whole, cells, cells, cells, P(), P(), P(), P(), P()),
        out_specs=whole,
        check_vma=False,
    )
```

time: 316 us -> 70.8 us (0.22)
  the two profiles are of different devices: /device:TPU:15 before, /device:TPU:104 now
where the time goes in v1:
time: 70.8 us; the launch traced here: 69.5 us
  Pallas kernels  35.3 us (50%)
  waiting for transfers between devices  18.3 us (26%)
  starting transfers between devices  11 us (16%)
  local copies, waits for them, and re-layouts  3.14 us (4%)
  other arithmetic  1.66 us (2%)
    pallas_call x1, Pallas kernels, stages(): pl.pallas_call(stages_kernel, name='stages', out_shape=jax.ShapeDtypeStru...  30.8 us
    ppermute x2, waiting for transfers between devices, exchange(): lax.ppermute(to_upper, axis, up)  17.6 us
    ppermute x2, starting transfers between devices, exchange(): lax.ppermute(to_lower, axis, down)  5.73 us
    ppermute x2, starting transfers between devices, exchange(): lax.ppermute(to_upper, axis, up)  5.24 us
    pallas_call x1, Pallas kernels, turn(): pl.pallas_call(turn_kernel, name='turn', out_shape=(jax.ShapeDtypeStruct(...  4.53 us
    unnamed x8, local copies, waits for them, and re-layouts  2.07 us
  transfers between devices with their start and end apart: 4, of which 3 were waited for; matrix products, arithmetic and copies ran while one was open for 0% of the time, Pallas kernels for 0%

profile of v1, /device:TPU:104, one launch (start us, length us, event | category | flops | bytes accessed | tf_op | source)
XLA Modules:
  0.0 69.5 jit_solution(10459293534806954319)
XLA Ops:
  0.0 0.0 copy-start
  0.0 0.9 %subtract_bitcast_fusion = s32[1,48,128]{2,1,0:T(8,128)S(1)} fusion(s32[48,128]{1,0:T(8,128)} %param.11), kind=kLoop, calls=%fused_computation.3 | loop fusion | flops 6144 | bytes 49152 | tf_op jit(solution)/shard_map/stack | solution.py:200
  0.9 0.8 %add_convert_fusion.m_ref = f32[3,48,128]{2,1,0:T(8,128)S(1)} fusion(s32[1,48,128]{2,1,0:T(8,128)} %bitcast.5, s32[1,48,128]{2,1,0:T(8,128)S(1)} %subtract_bitcast_fusion, s32[1,48,128]{2,1,0:T(8,128)} %bitcast.6), kind=kLoop, calls=%fused_computation.2 | loop fusion | flops 55296 | bytes 147456 | tf_op jit(solution)/shard_map/convert_element_type | solution.py:200
  1.6 1.1 %fusion = (f32[64,8,128]{2,1,0:T(8,128)S(1)}, f32[64,8,128]{2,1,0:T(8,128)S(1)}) fusion(f32[64,48,128]{2,1,0:T(8,128)} %x_ref.1), kind=kLoop, calls=%fused_computation.4 | loop fusion | bytes 1048576 | tf_op jit(solution)/shard_map/slice | solution.py:201
  2.7 3.3 %collective-permute-start = (f32[67,8,128]{2,1,0:T(8,128)S(1)}, f32[67,8,128]{2,1,0:T(8,128)S(1)}, u32[]{:S(2)}, u32[]{:S(2)}) collective-permute-start(f32[67,8,128]{2,1,0:T(8,128)S(1)} %pad_maximum_fusion), channel_id=1, source_target_pairs={{0,16},{16,32},{32,48},{48,64},{64,80},{80,96},{96,112},{1,17},{17... | collective-permute-start | bytes 823304 | tf_op jit(solution)/shard_map/ppermute | solution.py:193
  6.1 2.5 %collective-permute-start.1 = (f32[67,8,128]{2,1,0:T(8,128)S(1)}, f32[67,8,128]{2,1,0:T(8,128)S(1)}, u32[]{:S(2)}, u32[]{:S(2)}) collective-permute-start(f32[67,8,128]{2,1,0:T(8,128)S(1)} %pad_maximum_fusion.1), channel_id=1, source_target_pairs={{16,0},{32,16},{48,32},{64,48},{80,64},{96,80},{112,96},{17,1},{33... | collective-permute-start | bytes 823304 | tf_op jit(solution)/shard_map/ppermute | solution.py:193
  8.6 10.2 %collective-permute-done.top_ref = f32[67,8,128]{2,1,0:T(8,128)S(1)} collective-permute-done((f32[67,8,128]{2,1,0:T(8,128)S(1)}, f32[67,8,128]{2,1,0:T(8,128)S(1)}, u32[]{:S(2)}, u32[]{:S(2)}) %collective-permute-start) | collective-permute-done | bytes 274464 | tf_op jit(solution)/shard_map/ppermute | solution.py:193
  18.8 0.0 collective-permute-done.1.bot_ref
  18.8 0.0 copy-done
  18.8 4.5 %turn.1 = (f32[64,72,128]{2,1,0:T(8,128)S(1)}, f32[4,72,128]{2,1,0:T(8,128)S(1)}, f32[4,72,128]{2,1,0:T(8,128)S(1)}) custom-call(f32[64,48,128]{2,1,0:T(8,128)S(1)} %copy-done, f32[3,48,128]{2,1,0:T(8,128)S(1)} %add_convert_fusion.m_ref, f32[67,8,128]{2,1,0:T(8,128)S(1)} %collective-permute-done.top_ref, f32[67,8,128]{2,1,0:T(8,128)S(1)} %collective-permute-done.1.bot_ref), custom_call_target="tpu_custom_call" | custom-call | tf_op jit(solution)/shard_map/turn/pallas_call | solution.py:58
  23.4 0.0 copy-start.1
  23.4 1.4 %copy-done.1 = f32[64,72,128]{2,1,0:T(8,128)} copy-done((f32[64,72,128]{2,1,0:T(8,128)}, f32[64,72,128]{2,1,0:T(8,128)S(1)}, u32[]{:S(2)}) %copy-start.1) | copy-done | bytes 2359320
  24.8 3.2 %collective-permute-start.2 = (f32[4,72,128]{2,1,0:T(8,128)S(1)}, f32[4,72,128]{2,1,0:T(8,128)S(1)}, u32[]{:S(2)}, u32[]{:S(2)}) collective-permute-start(f32[4,72,128]{2,1,0:T(8,128)S(1)} %get-tuple-element.9), channel_id=1, source_target_pairs={{1,0},{2,1},{3,2},{4,3},{5,4},{6,5},{7,6},{8,7},{9,8},{10,9},{11,1... | collective-permute-start | bytes 442376 | tf_op jit(solution)/shard_map/ppermute | solution.py:193
  28.0 1.9 %collective-permute-start.3 = (f32[4,72,128]{2,1,0:T(8,128)S(1)}, f32[4,72,128]{2,1,0:T(8,128)S(1)}, u32[]{:S(2)}, u32[]{:S(2)}) collective-permute-start(f32[4,72,128]{2,1,0:T(8,128)S(1)} %get-tuple-element.10), channel_id=1, source_target_pairs={{0,1},{1,2},{2,3},{3,4},{4,5},{5,6},{6,7},{7,8},{8,9},{9,10},{10,1... | collective-permute-start | bytes 442376 | tf_op jit(solution)/shard_map/ppermute | solution.py:193
  29.9 0.7 %collective-permute-done.2.left_ref = f32[4,72,128]{2,1,0:T(8,128)S(1)} collective-permute-done((f32[4,72,128]{2,1,0:T(8,128)S(1)}, f32[4,72,128]{2,1,0:T(8,128)S(1)}, u32[]{:S(2)}, u32[]{:S(2)}) %collective-permute-start.2) | collective-permute-done | bytes 147488 | tf_op jit(solution)/shard_map/ppermute | solution.py:193
  30.6 0.0 copy-start.2
  30.6 7.4 %collective-permute-done.3.right_ref = f32[4,72,128]{2,1,0:T(8,128)S(1)} collective-permute-done((f32[4,72,128]{2,1,0:T(8,128)S(1)}, f32[4,72,128]{2,1,0:T(8,128)S(1)}, u32[]{:S(2)}, u32[]{:S(2)}) %collective-permute-start.3) | collective-permute-done | bytes 147488 | tf_op jit(solution)/shard_map/ppermute | solution.py:193
  38.1 0.0 copy-start.3
  38.1 0.0 copy-done.2
  38.1 0.7 copy-done.3
  38.7 30.8 %stages.1 = f32[64,48,128]{2,1,0:T(8,128)} custom-call(f32[64,72,128]{2,1,0:T(8,128)} %copy-done.1, f32[4,72,128]{2,1,0:T(8,128)} %copy-done.2, f32[4,72,128]{2,1,0:T(8,128)} %copy-done.3, f32[13,64]{1,0:T(8,128)} %rate_ref.1, f32[1,64]{1,0:T(1,128)} %bitcast.7, f32[64,64]{1,0:T(8,128)} %rows_ref.1, f32[64,64]{1,0:T(8,128)} %cols_ref.1, f32[64,64]{1,0:T(8,128)} %react_ref.1), custom_call_target="tpu_custom_call" | custom-call | tf_op jit(solution)/shard_map/stages/pallas_call | solution.py:172
  (3 shorter events, 0.0 us)
Async XLA Ops:
  0.0 18.8 %copy-start = (f32[64,48,128]{2,1,0:T(8,128)S(1)}, f32[64,48,128]{2,1,0:T(8,128)}, u32[]{:S(2)}) copy-start(f32[64,48,128]{2,1,0:T(8,128)} %x_ref.1) | copy-start | bytes 4718596
  2.7 16.1 %collective-permute-start = (f32[67,8,128]{2,1,0:T(8,128)S(1)}, f32[67,8,128]{2,1,0:T(8,128)S(1)}, u32[]{:S(2)}, u32[]{:S(2)}) collective-permute-start(f32[67,8,128]{2,1,0:T(8,128)S(1)} %pad_maximum_fusion), channel_id=1, source_target_pairs={{0,16},{16,32},{32,48},{48,64},{64,80},{80,96},{96,112},{1,17},{17... | collective-permute-start | bytes 823304 | tf_op jit(solution)/shard_map/ppermute | solution.py:193
  6.1 12.7 %collective-permute-start.1 = (f32[67,8,128]{2,1,0:T(8,128)S(1)}, f32[67,8,128]{2,1,0:T(8,128)S(1)}, u32[]{:S(2)}, u32[]{:S(2)}) collective-permute-start(f32[67,8,128]{2,1,0:T(8,128)S(1)} %pad_maximum_fusion.1), channel_id=1, source_target_pairs={{16,0},{32,16},{48,32},{64,48},{80,64},{96,80},{112,96},{17,1},{33... | collective-permute-start | bytes 823304 | tf_op jit(solution)/shard_map/ppermute | solution.py:193
  23.4 1.4 %copy-start.1 = (f32[64,72,128]{2,1,0:T(8,128)}, f32[64,72,128]{2,1,0:T(8,128)S(1)}, u32[]{:S(2)}) copy-start(f32[64,72,128]{2,1,0:T(8,128)S(1)} %get-tuple-element.8.f_ref) | copy-start | bytes 7077892
  24.8 5.9 %collective-permute-start.2 = (f32[4,72,128]{2,1,0:T(8,128)S(1)}, f32[4,72,128]{2,1,0:T(8,128)S(1)}, u32[]{:S(2)}, u32[]{:S(2)}) collective-permute-start(f32[4,72,128]{2,1,0:T(8,128)S(1)} %get-tuple-element.9), channel_id=1, source_target_pairs={{1,0},{2,1},{3,2},{4,3},{5,4},{6,5},{7,6},{8,7},{9,8},{10,9},{11,1... | collective-permute-start | bytes 442376 | tf_op jit(solution)/shard_map/ppermute | solution.py:193
  28.0 10.1 %collective-permute-start.3 = (f32[4,72,128]{2,1,0:T(8,128)S(1)}, f32[4,72,128]{2,1,0:T(8,128)S(1)}, u32[]{:S(2)}, u32[]{:S(2)}) collective-permute-start(f32[4,72,128]{2,1,0:T(8,128)S(1)} %get-tuple-element.10), channel_id=1, source_target_pairs={{0,1},{1,2},{2,3},{3,4},{4,5},{5,6},{6,7},{7,8},{8,9},{9,10},{10,1... | collective-permute-start | bytes 442376 | tf_op jit(solution)/shard_map/ppermute | solution.py:193
  30.6 7.4 %copy-start.2 = (f32[4,72,128]{2,1,0:T(8,128)}, f32[4,72,128]{2,1,0:T(8,128)S(1)}, u32[]{:S(2)}) copy-start(f32[4,72,128]{2,1,0:T(8,128)S(1)} %collective-permute-done.2.left_ref) | copy-start | bytes 442372
  38.1 0.7 copy-start.3

commit v2 on v0

v2 whole, which is shorter than its diff:
```python
import jax
import jax.numpy as jnp
from jax import lax
from jax.experimental import pallas as pl
from jax.experimental.pallas import tpu as pltpu
from jax.sharding import PartitionSpec as P

ITERS = 4
STAGES = 2 * ITERS
HALO = STAGES
C, ROWS, COLS = 64, 48, 128
HEIGHT = ROWS + 2 * HALO
WIDTH = COLS + 2 * HALO
TILES = HEIGHT // 2
OWN = TILES - HALO
LANES = 2 * C
GROUP = 8
MSG = 4 * WIDTH
BF = jnp.bfloat16
F32 = jnp.float32


def split(x):
    hi = x.astype(BF)
    return hi, (x - hi.astype(F32)).astype(BF)


def lanes(shape):
    return lax.broadcasted_iota(jnp.int32, shape, len(shape) - 1)


def call(kernel, name, outs, scratch=(), limit=12):
    return pl.pallas_call(
        kernel,
        name=name,
        out_shape=[jax.ShapeDtypeStruct(s, d) for s, d in outs],
        scratch_shapes=[pltpu.VMEM(s, d) for s, d in scratch],
        compiler_params=pltpu.CompilerParams(vmem_limit_bytes=limit * 2**20),
    )


FUEL, BURN, LIT = 0, HEIGHT, 2 * HEIGHT


def pack_kernel(x_ref, fuel_ref, break_ref, lit_ref, field_ref, masks_ref, left_ref, right_ref):
    masks_ref[...] = jnp.zeros_like(masks_ref)
    masks_ref[FUEL + HALO : FUEL + HALO + ROWS] = fuel_ref[...].astype(F32)
    masks_ref[BURN + HALO : BURN + HALO + ROWS] = (1 - break_ref[...]).astype(F32)
    masks_ref[LIT + HALO : LIT + HALO + ROWS] = lit_ref[...].astype(F32)
    flat = x_ref.reshape(C * ROWS, COLS)

    def messages(k, turned):
        left_ref[k] = turned[0:HALO]
        right_ref[k] = turned[COLS - HALO :]

    for k in range(OWN):
        top = flat[pl.ds(k, C, stride=ROWS), :]
        bottom = flat[pl.ds(ROWS - 1 - k, C, stride=ROWS), :]
        turned = jnp.concatenate([top, bottom], 0).T
        field_ref[k] = turned
        messages(k, turned)
    messages(OWN, masks_ref[0:128].T)
    messages(OWN + 1, masks_ref[128:256].T)


def pack(x, fuel, firebreak, lit):
    message = ((OWN + 2, HALO, LANES), F32)
    return call(
        pack_kernel, "pack", [((OWN, COLS, LANES), F32), ((256, COLS), F32), message, message]
    )(x, fuel, firebreak, lit)


def onehot(fuel, burn, lit):
    slot = lax.broadcasted_iota(jnp.int32, (C, 128), 0)
    cls = (slot & 15).astype(F32)
    halves = []
    for f, b, i in zip(fuel, burn, lit):
        picked = jnp.where((cls == f) | (cls == 13.0), b, jnp.where(cls == 14.0, b * i, 0.0))
        halves.append(jnp.where(slot < 32, picked, 0.0))
    return jnp.concatenate(halves, 0)


def rates_kernel(
    masks_ref, rate_ref, heat_ref, rows_ref, cols_ref, react_ref,
    brate_ref, burn_ref, bheat_ref, table_ref, w1_ref, w2_ref, w3_ref, tab,
):
    tab[...] = jnp.zeros_like(tab)
    tab[0:13, 0:64] = rate_ref[...]
    tab[14:15, 0:64] = heat_ref[...]
    t = tab[...]
    t = t + pltpu.roll(t, 64, 1)
    row = lax.broadcasted_iota(jnp.int32, (16, 128), 0)
    h = jnp.concatenate(
        [jnp.where(row < 13, t, 0.0), jnp.where(row == 13, 1.0, 0.0), jnp.where(row == 14, t, 0.0)], 1
    )
    hi, lo = split(h)
    half = jnp.concatenate([hi.astype(F32), lo.astype(F32), jnp.zeros((32, 384), F32)], 0)
    low = (lanes((64, 384)) & 127) < 64
    table_ref[...] = jnp.concatenate([jnp.where(low, half, 0.0), jnp.where(low, 0.0, half)], 0).astype(BF)

    zero = jnp.zeros((C, C), F32)
    eye = jnp.where(lax.broadcasted_iota(jnp.int32, (C, C), 0) == lanes((C, C)), 1.0, 0.0)

    def both(m):
        return split(jnp.concatenate([jnp.concatenate([m, zero], 1), jnp.concatenate([zero, m], 1)], 0).T)

    r_hi, r_lo = both(rows_ref[...] + eye)
    c_hi, c_lo = both(cols_ref[...] + eye)
    e_hi, e_lo = both(react_ref[...])
    w1_ref[...] = jnp.concatenate([jnp.concatenate([r_hi, c_hi], 1)] * 2, 0)
    w2_ref[...] = jnp.concatenate([r_lo, c_lo], 1)
    w3_ref[...] = jnp.concatenate(
        [jnp.concatenate([e_hi, e_lo], 1), jnp.concatenate([e_hi, jnp.zeros((128, 128), BF)], 1)], 0
    )
    for r in range(HALO, TILES):
        put_rates(masks_ref, table_ref, r, brate_ref, burn_ref, bheat_ref)


def put_rates(masks_ref, table_ref, r, brate_ref, burn_ref, bheat_ref):
    pick = lambda base: (masks_ref[base + r : base + r + 1], masks_ref[base + 63 - r : base + 64 - r])
    hot = onehot(pick(FUEL), pick(BURN), pick(LIT)).T.astype(BF)
    got = jnp.dot(hot, table_ref[...], preferred_element_type=F32)
    at = slice(HALO, HALO + COLS)
    brate_ref[r, at], burn_ref[r, at], bheat_ref[r, at] = got[:, 0:128], got[:, 128:256], got[:, 256:384]


def put_edge_rates(edge_ref, table_ref, r0, brate_ref, burn_ref, bheat_ref):
    rows = []
    for base in (FUEL, BURN, LIT):
        halves = []
        for h in range(2):
            total = None
            for k in range(8):
                p = r0 + k if h == 0 else 63 - r0 - k
                part = edge_ref[base + p : base + p + 1]
                part = pltpu.roll(part, 16 * k, 1) if k else part
                total = part if total is None else total + part
            halves.append(total)
        rows.append(halves)
    got = jnp.dot(onehot(*rows).T.astype(BF), table_ref[...], preferred_element_type=F32)
    for k in range(8):
        for side, at in ((0, slice(0, HALO)), (8, slice(HALO + COLS, WIDTH))):
            part = got[16 * k + side : 16 * k + side + 8]
            r = r0 + k
            brate_ref[r, at], burn_ref[r, at], bheat_ref[r, at] = part[:, 0:128], part[:, 128:256], part[:, 256:384]


def rates(masks, rate, heat, rows, cols, react):
    cells = ((TILES, WIDTH, LANES), F32)
    return call(
        rates_kernel, "rates",
        [cells, cells, cells, ((128, 384), BF), ((256, 256), BF), ((128, 256), BF), ((256, 256), BF)],
        [((16, 128), F32)],
    )(masks, rate, heat, rows, cols, react)


def turned_edges(left_ref, right_ref, k):
    both = jnp.concatenate([left_ref[k], right_ref[k], jnp.zeros((112, 128), F32)], 0)
    return both.T


def rows_kernel(field_ref, masks_ref, left_ref, right_ref, up_ref, down_ref, edge_ref):
    low = lanes((WIDTH, LANES)) < C

    def tile(k):
        return jnp.concatenate([left_ref[k], field_ref[k], right_ref[k]], 0)

    for t in range(4):
        near, far = tile(t), pltpu.roll(tile(4 + t), C, 1)
        at = slice(t * WIDTH, (t + 1) * WIDTH)
        up_ref[at] = jnp.where(low, near, far)
        down_ref[at] = jnp.where(low, far, near)
    edge_ref[0:128] = turned_edges(left_ref, right_ref, OWN)
    edge_ref[128:256] = turned_edges(left_ref, right_ref, OWN + 1)
    for i, base in enumerate((FUEL, BURN, LIT)):
        for ref, first in ((up_ref, HALO), (down_ref, HALO + ROWS - 8)):
            rows = slice(base + first, base + first + 8)
            ref[MSG + 8 * i : MSG + 8 * i + 8] = masks_ref[rows]
            ref[MSG + 24 + 8 * i : MSG + 32 + 8 * i] = edge_ref[rows]


def row_messages(field, masks, left, right):
    message = ((MSG + 48, LANES), F32)
    return call(rows_kernel, "rows", [message, message, ((256, LANES), F32)])(field, masks, left, right)


def sweep(src, dst, base, first, last, second, rate_of, weights, S, W, T):
    w1, w2, w3 = weights
    brate, burn, bheat = rate_of

    def mix(r, n):
        x = src[r - base : r - base + n].reshape(n * WIDTH, LANES)
        hi, lo = split(x)
        t_hi, t_lo = split(jnp.tanh(x))
        sw = jnp.dot(jnp.concatenate([hi, lo], 1), w1[...], preferred_element_type=F32)
        sw = sw + jnp.dot(hi, w2[...], preferred_element_type=F32)
        tt = jnp.dot(jnp.concatenate([t_hi, t_lo], 1), w3[...], preferred_element_type=F32)
        tt = tt[:, 0:LANES] + tt[:, LANES:]
        for k in range(n):
            at = slice(k * WIDTH, (k + 1) * WIDTH)
            q = r + k
            S[q - base] = sw[at, 0:LANES]
            W[q - base, 8 : 8 + WIDTH] = sw[at, LANES:]
            if first <= q < last:
                T[q - base] = 0.5 * x[at] + (burn(q) * tt[at] + bheat(q))
            if q == TILES - 1:
                S[q - base + 1] = pltpu.roll(sw[at, 0:LANES], C, 1)

    def post(r):
        q = r - base
        centre = S[q] + W[q, 8 : 8 + WIDTH]
        around = (S[q - 1] + S[q + 1]) + (W[q, 7 : 7 + WIDTH] + W[q, 9 : 9 + WIDTH])
        g = T[q] + brate(r) * (around - centre - centre)
        dst[q] = 0.5 * (dst[q] + g) if second else g

    end = min(last + 1, TILES)
    r, todo = first - 1, first
    while r < end:
        n = min(GROUP, end - r)
        if 0 < end - r - n < 3:
            n = end - r
        mix(r, n)
        r += n
        limit = last if r == end else min(last, r - 1)
        for q in range(todo, limit):
            post(q)
        todo = max(todo, limit)


def inner_kernel(
    field_ref, left_ref, right_ref, edge_ref, brate_in, burn_in, bheat_in, table_ref, w1, w2, w3,
    A, B, brate, burn, bheat, S, W, T,
):
    for k in range(OWN):
        A[HALO + k, 0:HALO] = left_ref[k]
        A[HALO + k, HALO : HALO + COLS] = field_ref[k]
        A[HALO + k, HALO + COLS :] = right_ref[k]
    W[...] = jnp.zeros_like(W)
    at = slice(HALO, HALO + COLS)
    for r in range(HALO, TILES):
        brate[r, at], burn[r, at], bheat[r, at] = brate_in[r, at], burn_in[r, at], bheat_in[r, at]
    for r0 in range(HALO, TILES, 8):
        put_edge_rates(edge_ref, table_ref, r0, brate, burn, bheat)
    rate_of = [lambda r, ref=ref: ref[r] for ref in (brate, burn, bheat)]
    for s in range(1, STAGES + 1):
        src, dst = (A, B) if s % 2 else (B, A)
        sweep(src, dst, 0, HALO + s, TILES, s % 2 == 0, rate_of, (w1, w2, w3), S, W, T)


def inner(field, left, right, edge, rate_arrays):
    cells = ((TILES, WIDTH, LANES), F32)
    return call(
        inner_kernel, "inner", [cells] * 5,
        [((TILES + 1, WIDTH, LANES), F32), ((TILES, WIDTH + 16, LANES), F32), ((TILES, WIDTH, LANES), F32)],
    )(field, left, right, edge, *rate_arrays)


def outer_kernel(
    A_in, B_in, brate_in, burn_in, bheat_in, top_ref, bottom_ref, table_ref, w1, w2, w3,
    out_ref, A, B, brate, burn, bheat, masks, edge, S, W, T,
):
    low = lanes((WIDTH, LANES)) < C
    for t in range(4):
        at = slice(t * WIDTH, (t + 1) * WIDTH)
        A[7 - t] = pltpu.roll(jnp.where(low, bottom_ref[at], top_ref[at]), C, 1)
        A[3 - t] = jnp.where(low, top_ref[at], bottom_ref[at])
    for r in range(7, 18):
        if r > 7:
            A[r] = A_in[r]
        B[r] = B_in[r]
    W[...] = jnp.zeros_like(W)
    for i, base in enumerate((FUEL, BURN, LIT)):
        for ref, first in ((top_ref, 0), (bottom_ref, HALO + ROWS)):
            rows = slice(base + first, base + first + 8)
            masks[rows] = ref[MSG + 8 * i : MSG + 8 * i + 8]
            edge[rows] = ref[MSG + 24 + 8 * i : MSG + 32 + 8 * i]
    for r in range(HALO):
        put_rates(masks, table_ref, r, brate, burn, bheat)
    put_edge_rates(edge, table_ref, 0, brate, burn, bheat)
    rate_of = [
        lambda r, near=near, far=far: near[r] if r < HALO else far[r]
        for near, far in ((brate, brate_in), (burn, burn_in), (bheat, bheat_in))
    ]
    for s in range(1, STAGES + 1):
        src, dst = (A, B) if s % 2 else (B, A)
        sweep(src, dst, 0, s, HALO + s, s % 2 == 0, rate_of, (w1, w2, w3), S, W, T)
    flat = out_ref.reshape(C * ROWS, COLS)
    for k in range(OWN):
        r = HALO + k
        turned = (A if r < 2 * HALO else A_in)[r, HALO : HALO + COLS].T
        flat[pl.ds(k, C, stride=ROWS), :] = turned[0:C]
        flat[pl.ds(ROWS - 1 - k, C, stride=ROWS), :] = turned[C:]


def outer(A, B, brate, burn, bheat, top, bottom, weights):
    few = 18
    cells = ((few, WIDTH, LANES), F32)
    edge_cells = ((HALO, WIDTH, LANES), F32)
    return call(
        outer_kernel, "outer", [((C, ROWS, COLS), F32)],
        [cells, cells, edge_cells, edge_cells, edge_cells, ((192, COLS), F32), ((192, COLS), F32),
         cells, ((few, WIDTH + 16, LANES), F32), cells],
    )(A, B, brate, burn, bheat, top, bottom, *weights)[0]


def exchange(to_lower, to_upper, axis):
    up = [(i, i + 1) for i in range(lax.axis_size(axis) - 1)]
    down = [(b, a) for a, b in up]
    return lax.ppermute(to_lower, axis, down), lax.ppermute(to_upper, axis, up)


def per_device(
    fire_state, fuel_class, firebreak, ignition,
    spread_rate, spread_rows, spread_cols, reaction, ignition_heat,
):
    field, masks, first, last = pack(fire_state, fuel_class, firebreak, ignition)
    right, left = exchange(first, last, "col")
    rate_arrays = rates(masks, spread_rate, ignition_heat[None], spread_rows, spread_cols, reaction)
    up, down, edge = row_messages(field, masks, left, right)
    bottom, top = exchange(up, down, "row")
    A, B, brate, burn, bheat = inner(field, left, right, edge, rate_arrays)
    return outer(A, B, brate, burn, bheat, top, bottom, rate_arrays[3:])


def solution(mesh):
    whole = P(None, "row", "col")
    cells = P("row", "col")
    return jax.shard_map(
        per_device,
        mesh=mesh,
        in_specs=(whole, cells, cells, cells, P(), P(), P(), P(), P()),
        out_specs=whole,
        check_vma=False,
    )
```

time: 316 us -> 47 us (0.15); the launches traced: 312 us -> 46.6 us
  starting transfers between devices: 119 us -> 14.1 us
  matrix products: 95.6 us -> 0 us
  local copies, waits for them, and re-layouts: 77.2 us -> 3.64 us
  Pallas kernels: 0 us -> 21 us
  waiting for transfers between devices: 19 us -> 7.81 us
    ppermute x32 -> x4, starting transfers between devices: 119 us -> 14.1 us  [the longest x2 9.7 us: exchange(): lax.ppermute(to_upper, axis, up)]
    dot_general x25 -> x0, matrix products: 95.6 us -> none  [the longest x24 93.7 us: mixing(): jnp.einsum('dc,chw->dhw', matrix, values, precision=lax.Precision.HIGHEST)]
    slice x30 -> x0, local copies, waits for them, and re-layouts: 39.2 us -> none  [the longest x23 29.9 us: with_halo(): last = lax.slice_in_dim(x, length - width, length, axis=dim)]
    ppermute x16 -> x0, local copies, waits for them, and re-layouts: 27.4 us -> none  [the longest x8 13.8 us: with_halo(): lax.ppermute(last, axis, up)]
    pallas_call x0 -> x5, Pallas kernels: none -> 21 us  [the longest x1 12.1 us: inner(): call(inner_kernel, 'inner', [cells] * 5, [((TILES + 1, WIDTH, LANES), F32...]
    ppermute x32 -> x4, waiting for transfers between devices: 19 us -> 7.81 us  [the longest x2 7.81 us: exchange(): lax.ppermute(to_lower, axis, down)]
    unnamed x91 -> x18, local copies, waits for them, and re-layouts: 8.22 us -> 3.64 us
  transfers between devices with their start and end apart: 32 -> 4, of which waited for: 4 -> 1; matrix products, arithmetic and copies ran while one was open for 26% -> 0% of each run, Pallas kernels for 0% -> 28%
where the time goes in v2:
time: 47 us; the launch traced here: 46.6 us
  Pallas kernels  21 us (45%)
  starting transfers between devices  14.1 us (30%)
  waiting for transfers between devices  7.81 us (17%)
  local copies, waits for them, and re-layouts  3.64 us (8%)
    pallas_call x1, Pallas kernels, inner(): call(inner_kernel, 'inner', [cells] * 5, [((TILES + 1, WIDTH, LANES), F32...  12.1 us
    ppermute x2, starting transfers between devices, exchange(): lax.ppermute(to_upper, axis, up)  9.7 us
    ppermute x2, waiting for transfers between devices, exchange(): lax.ppermute(to_lower, axis, down)  7.81 us
    pallas_call x1, Pallas kernels, outer(): call(outer_kernel, 'outer', [((C, ROWS, COLS), F32)], [cells, cells, edge...  7.27 us
    ppermute x2, starting transfers between devices, exchange(): lax.ppermute(to_lower, axis, down)  4.39 us
    unnamed x18, local copies, waits for them, and re-layouts  3.64 us
  transfers between devices with their start and end apart: 4, of which 1 were waited for; matrix products, arithmetic and copies ran while one was open for 0% of the time, Pallas kernels for 28%

profile of v2, /device:TPU:15, one launch (start us, length us, event | category | flops | bytes accessed | tf_op | source)
XLA Modules:
  0.0 46.6 jit_solution(13544054565396888378)
XLA Ops:
  0.0 0.0 copy-start
  0.0 1.4 %copy-done = f32[64,48,128]{2,1,0:T(8,128)S(1)} copy-done((f32[64,48,128]{2,1,0:T(8,128)S(1)}, f32[64,48,128]{2,1,0:T(8,128)}, u32[]{:S(2)}) %copy-start) | copy-done | bytes 1572888
  1.4 0.0 copy-start.4
  1.4 0.7 %copy-done.4 = s32[48,128]{1,0:T(8,128)S(1)} copy-done((s32[48,128]{1,0:T(8,128)S(1)}, s32[48,128]{1,0:T(8,128)}, u32[]{:S(2)}) %copy-start.4) | copy-done | bytes 24600
  2.1 0.0 copy-start.5
  2.1 0.7 %copy-done.5 = s32[48,128]{1,0:T(8,128)S(1)} copy-done((s32[48,128]{1,0:T(8,128)S(1)}, s32[48,128]{1,0:T(8,128)}, u32[]{:S(2)}) %copy-start.5) | copy-done | bytes 24600
  2.9 0.0 copy-start.6
  2.9 0.7 %copy-done.6 = s32[48,128]{1,0:T(8,128)S(1)} copy-done((s32[48,128]{1,0:T(8,128)S(1)}, s32[48,128]{1,0:T(8,128)}, u32[]{:S(2)}) %copy-start.6) | copy-done | bytes 24600
  3.6 0.0 copy-start.1
  3.6 0.0 copy-start.2
  3.6 0.0 copy-start.3
  3.6 0.0 copy-start.7
  3.6 0.0 copy-start.8
  3.6 0.5 %pack.1 = (f32[24,128,128]{2,1,0:T(8,128)S(1)}, f32[256,128]{1,0:T(8,128)S(1)}, f32[26,8,128]{2,1,0:T(8,128)S(1)}, f32[26,8,128]{2,1,0:T(8,128)S(1)}) custom-call(f32[64,48,128]{2,1,0:T(8,128)S(1)} %copy-done, s32[48,128]{1,0:T(8,128)S(1)} %copy-done.4, s32[48,128]{1,0:T(8,128)S(1)} %copy-done.5, s32[48,128]{1,0:T(8,128)S(1)} %copy-done.6), custom_call_target="tpu_custom_call" | custom-call | tf_op jit(solution)/shard_map/pack/pallas_call | solution.py:68
  4.2 6.0 %collective-permute-start = (f32[26,8,128]{2,1,0:T(8,128)S(1)}, f32[26,8,128]{2,1,0:T(8,128)S(1)}, u32[]{:S(2)}, u32[]{:S(2)}) collective-permute-start(f32[26,8,128]{2,1,0:T(8,128)S(1)} %get-tuple-element.25), channel_id=1, source_target_pairs={{0,1},{1,2},{2,3},{3,4},{4,5},{5,6},{6,7},{7,8},{8,9},{9,10},{10,1... | collective-permute-start | bytes 319496 | tf_op jit(solution)/shard_map/ppermute | solution.py:309
  10.2 1.9 %collective-permute-start.1 = (f32[26,8,128]{2,1,0:T(8,128)S(1)}, f32[26,8,128]{2,1,0:T(8,128)S(1)}, u32[]{:S(2)}, u32[]{:S(2)}) collective-permute-start(f32[26,8,128]{2,1,0:T(8,128)S(1)} %get-tuple-element.26), channel_id=1, source_target_pairs={{1,0},{2,1},{3,2},{4,3},{5,4},{6,5},{7,6},{8,7},{9,8},{10,9},{11,1... | collective-permute-start | bytes 319496 | tf_op jit(solution)/shard_map/ppermute | solution.py:309
  12.1 0.0 collective-permute-done.left_ref
  12.1 7.8 %collective-permute-done.1.right_ref = f32[26,8,128]{2,1,0:T(8,128)S(1)} collective-permute-done((f32[26,8,128]{2,1,0:T(8,128)S(1)}, f32[26,8,128]{2,1,0:T(8,128)S(1)}, u32[]{:S(2)}, u32[]{:S(2)}) %collective-permute-start.1) | collective-permute-done | bytes 106528 | tf_op jit(solution)/shard_map/ppermute | solution.py:309
  19.9 0.2 rows.1
  20.1 3.7 %collective-permute-start.2 = (f32[624,128]{1,0:T(8,128)S(1)}, f32[624,128]{1,0:T(8,128)S(1)}, u32[]{:S(2)}, u32[]{:S(2)}) collective-permute-start(f32[624,128]{1,0:T(8,128)S(1)} %get-tuple-element.41), channel_id=1, source_target_pairs={{0,16},{16,32},{32,48},{48,64},{64,80},{80,96},{96,112},{1,17},{17... | collective-permute-start | bytes 958472 | tf_op jit(solution)/shard_map/ppermute | solution.py:309
  23.9 2.5 %collective-permute-start.3 = (f32[624,128]{1,0:T(8,128)S(1)}, f32[624,128]{1,0:T(8,128)S(1)}, u32[]{:S(2)}, u32[]{:S(2)}) collective-permute-start(f32[624,128]{1,0:T(8,128)S(1)} %get-tuple-element.42), channel_id=1, source_target_pairs={{16,0},{32,16},{48,32},{64,48},{80,64},{96,80},{112,96},{17,1},{33... | collective-permute-start | bytes 958472 | tf_op jit(solution)/shard_map/ppermute | solution.py:309
  26.3 0.0 copy-done.1
  26.3 0.0 copy-done.2
  26.4 0.0 copy-done.3
  26.4 0.0 copy-done.7
  26.4 0.0 copy-done.8
  26.4 0.9 %rates.1 = (f32[32,144,128]{2,1,0:T(8,128)S(1)}, f32[32,144,128]{2,1,0:T(8,128)S(1)}, f32[32,144,128]{2,1,0:T(8,128)S(1)}, bf16[128,384]{1,0:T(8,128)(2,1)S(1)},...) custom-call(f32[256,128]{1,0:T(8,128)S(1)} %get-tuple-element.27.masks_ref, ...), custom_call_target="tpu_custom_call" | custom-call | tf_op jit(solution)/shard_map/rates/pallas_call | solution.py:150
  27.2 12.1 %inner.1 = (f32[32,144,128]{2,1,0:T(8,128)S(1)}, f32[32,144,128]{2,1,0:T(8,128)S(1)}, f32[32,144,128]{2,1,0:T(8,128)S(1)}, f32[32,144,128]{2,1,0:T(8,128)S(1)}, f32[32,144,128]{2,1,0:T(8,128)S(1)}) custom-call(f32[24,128,128]{2,1,0:T(8,128)S(1)} %get-tuple-element.24.field_ref, f32[26,8,128]{2,1,0:T(8,128)S(1)} %collective-permute-done.left_ref, ...), custom_call_target="tpu_custom_call" | custom-call | tf_op jit(solution)/shard_map/inner/pallas_call | solution.py:252
  39.4 0.0 collective-permute-done.2.top_ref
  39.4 0.0 collective-permute-done.3.bottom_ref
  39.4 7.3 %outer.1 = f32[64,48,128]{2,1,0:T(8,128)} custom-call(f32[32,144,128]{2,1,0:T(8,128)S(1)} %get-tuple-element.36.A_in, f32[32,144,128]{2,1,0:T(8,128)S(1)} %get-tuple-element.37.B_in, f32[32,144,128]{2,1,0:T(8,128)S(1)} %get-tuple-element.38.brate_in, f32[32,144,128]{2,1,0:T(8,128)S(1)} %get-tuple-element.39.burn_in, ...), custom_call_target="tpu_custom_call" | custom-call | tf_op jit(solution)/shard_map/outer/pallas_call | solution.py:299
Async XLA Ops:
  0.0 1.4 %copy-start = (f32[64,48,128]{2,1,0:T(8,128)S(1)}, f32[64,48,128]{2,1,0:T(8,128)}, u32[]{:S(2)}) copy-start(f32[64,48,128]{2,1,0:T(8,128)} %x_ref.1) | copy-start | bytes 4718596
  1.4 0.7 %copy-start.4 = (s32[48,128]{1,0:T(8,128)S(1)}, s32[48,128]{1,0:T(8,128)}, u32[]{:S(2)}) copy-start(s32[48,128]{1,0:T(8,128)} %fuel_ref.1) | copy-start | bytes 73732
  2.1 0.7 %copy-start.5 = (s32[48,128]{1,0:T(8,128)S(1)}, s32[48,128]{1,0:T(8,128)}, u32[]{:S(2)}) copy-start(s32[48,128]{1,0:T(8,128)} %break_ref.1) | copy-start | bytes 73732
  2.9 0.7 %copy-start.6 = (s32[48,128]{1,0:T(8,128)S(1)}, s32[48,128]{1,0:T(8,128)}, u32[]{:S(2)}) copy-start(s32[48,128]{1,0:T(8,128)} %lit_ref.1) | copy-start | bytes 73732
  3.6 22.7 %copy-start.1 = (f32[64,64]{1,0:T(8,128)S(1)}, f32[64,64]{1,0:T(8,128)}, u32[]{:S(2)}) copy-start(f32[64,64]{1,0:T(8,128)} %rows_ref.1) | copy-start | bytes 49156
  3.6 22.7 %copy-start.2 = (f32[64,64]{1,0:T(8,128)S(1)}, f32[64,64]{1,0:T(8,128)}, u32[]{:S(2)}) copy-start(f32[64,64]{1,0:T(8,128)} %cols_ref.1) | copy-start | bytes 49156
  3.6 22.7 %copy-start.3 = (f32[64,64]{1,0:T(8,128)S(1)}, f32[64,64]{1,0:T(8,128)}, u32[]{:S(2)}) copy-start(f32[64,64]{1,0:T(8,128)} %react_ref.1) | copy-start | bytes 49156
  3.6 22.7 %copy-start.7 = (f32[13,64]{1,0:T(8,128)S(1)}, f32[13,64]{1,0:T(8,128)}, u32[]{:S(2)}) copy-start(f32[13,64]{1,0:T(8,128)} %rate_ref.1) | copy-start | bytes 9988
  3.6 22.7 %copy-start.8 = (f32[64]{0:T(128)S(1)}, f32[64]{0:T(128)}, u32[]{:S(2)}) copy-start(f32[64]{0:T(128)} %param.17) | copy-start | bytes 772
  4.2 7.9 %collective-permute-start = (f32[26,8,128]{2,1,0:T(8,128)S(1)}, f32[26,8,128]{2,1,0:T(8,128)S(1)}, u32[]{:S(2)}, u32[]{:S(2)}) collective-permute-start(f32[26,8,128]{2,1,0:T(8,128)S(1)} %get-tuple-element.25), channel_id=1, source_target_pairs={{0,1},{1,2},{2,3},{3,4},{4,5},{5,6},{6,7},{7,8},{8,9},{9,10},{10,1... | collective-permute-start | bytes 319496 | tf_op jit(solution)/shard_map/ppermute | solution.py:309
  10.2 9.7 %collective-permute-start.1 = (f32[26,8,128]{2,1,0:T(8,128)S(1)}, f32[26,8,128]{2,1,0:T(8,128)S(1)}, u32[]{:S(2)}, u32[]{:S(2)}) collective-permute-start(f32[26,8,128]{2,1,0:T(8,128)S(1)} %get-tuple-element.26), channel_id=1, source_target_pairs={{1,0},{2,1},{3,2},{4,3},{5,4},{6,5},{7,6},{8,7},{9,8},{10,9},{11,1... | collective-permute-start | bytes 319496 | tf_op jit(solution)/shard_map/ppermute | solution.py:309
  20.1 19.2 %collective-permute-start.2 = (f32[624,128]{1,0:T(8,128)S(1)}, f32[624,128]{1,0:T(8,128)S(1)}, u32[]{:S(2)}, u32[]{:S(2)}) collective-permute-start(f32[624,128]{1,0:T(8,128)S(1)} %get-tuple-element.41), channel_id=1, source_target_pairs={{0,16},{16,32},{32,48},{48,64},{64,80},{80,96},{96,112},{1,17},{17... | collective-permute-start | bytes 958472 | tf_op jit(solution)/shard_map/ppermute | solution.py:309
  23.9 15.5 %collective-permute-start.3 = (f32[624,128]{1,0:T(8,128)S(1)}, f32[624,128]{1,0:T(8,128)S(1)}, u32[]{:S(2)}, u32[]{:S(2)}) collective-permute-start(f32[624,128]{1,0:T(8,128)S(1)} %get-tuple-element.42), channel_id=1, source_target_pairs={{16,0},{32,16},{48,32},{64,48},{80,64},{96,80},{112,96},{17,1},{33... | collective-permute-start | bytes 958472 | tf_op jit(solution)/shard_map/ppermute | solution.py:309

commit v3 on v2

v3 whole, which is shorter than its diff:
```python
import jax
import jax.numpy as jnp
from jax import lax
from jax.experimental import pallas as pl
from jax.experimental.pallas import tpu as pltpu
from jax.sharding import PartitionSpec as P

ITERS = 4
STAGES = 2 * ITERS
HALO = STAGES
C, ROWS, COLS = 64, 48, 128
HEIGHT = ROWS + 2 * HALO
WIDTH = COLS + 2 * HALO
TILES = HEIGHT // 2
OWN = TILES - HALO
LANES = 2 * C
INNER_GROUP = 8
OUTER_GROUP = 4
MSG = 4 * WIDTH
BF = jnp.bfloat16
F32 = jnp.float32


def split(x):
    hi = x.astype(BF)
    return hi, (x - hi.astype(F32)).astype(BF)


def lanes(shape):
    return lax.broadcasted_iota(jnp.int32, shape, len(shape) - 1)


def call(kernel, name, outs, scratch=(), limit=12, from_hbm=0, extra=()):
    specs = {"in_specs": [pl.BlockSpec(memory_space=pltpu.HBM)] * from_hbm} if from_hbm else {}
    return pl.pallas_call(
        kernel,
        name=name,
        out_shape=[jax.ShapeDtypeStruct(s, d) for s, d in outs],
        scratch_shapes=[pltpu.VMEM(s, d) for s, d in scratch] + list(extra),
        **specs,
        compiler_params=pltpu.CompilerParams(vmem_limit_bytes=limit * 2**20),
    )


FUEL, BURN, LIT = 0, HEIGHT, 2 * HEIGHT


def even(axis):
    return lax.rem(lax.axis_index(axis), 2) == 0


def pack_kernel(
    x_hbm, fuel_hbm, break_hbm, lit_hbm, field_ref, masks_ref, near_ref, far_ref, x_ref, ints, sems
):
    copies = [
        pltpu.make_async_copy(x_hbm.at[:, pl.ds(8 * g, 8), :], x_ref.at[:, pl.ds(8 * g, 8), :], sems.at[g])
        for g in range(ROWS // 8)
    ]
    for g in (0, 5, 1, 4, 2, 3):
        copies[g].start()
    small = [
        pltpu.make_async_copy(ref, ints.at[i], sems.at[6 + i])
        for i, ref in enumerate((fuel_hbm, break_hbm, lit_hbm))
    ]
    for copy in small:
        copy.start()
    masks_ref[...] = jnp.zeros_like(masks_ref)
    flat = x_ref.reshape(C * ROWS, COLS)
    is_even = even("col")

    def messages(k, turned):
        first, last = turned[0:HALO], turned[COLS - HALO :]
        near_ref[k] = jnp.where(is_even, last, first)
        far_ref[k] = jnp.where(is_even, first, last)

    for k in range(OWN):
        if k % 8 == 0:
            copies[k // 8].wait()
            copies[5 - k // 8].wait()
        top = flat[pl.ds(k, C, stride=ROWS), :]
        bottom = flat[pl.ds(ROWS - 1 - k, C, stride=ROWS), :]
        turned = jnp.concatenate([top, bottom], 0).T
        field_ref[k] = turned
        messages(k, turned)
    for copy in small:
        copy.wait()
    masks_ref[FUEL + HALO : FUEL + HALO + ROWS] = ints[0].astype(F32)
    masks_ref[BURN + HALO : BURN + HALO + ROWS] = (1 - ints[1]).astype(F32)
    masks_ref[LIT + HALO : LIT + HALO + ROWS] = ints[2].astype(F32)
    messages(OWN, masks_ref[0:128].T)
    messages(OWN + 1, masks_ref[128:256].T)


def pack(x, fuel, firebreak, lit):
    message = ((OWN + 2, HALO, LANES), F32)
    return call(
        pack_kernel, "pack", [((OWN, COLS, LANES), F32), ((256, COLS), F32), message, message],
        [((C, ROWS, COLS), F32)], from_hbm=4,
        extra=[pltpu.VMEM((3, ROWS, COLS), jnp.int32), pltpu.SemaphoreType.DMA((9,))],
    )(x, fuel, firebreak, lit)


def onehot(fuel, burn, lit):
    slot = lax.broadcasted_iota(jnp.int32, (C, 128), 0)
    cls = (slot & 15).astype(F32)
    halves = []
    for f, b, i in zip(fuel, burn, lit):
        picked = jnp.where((cls == f) | (cls == 13.0), b, jnp.where(cls == 14.0, b * i, 0.0))
        halves.append(jnp.where(slot < 32, picked, 0.0))
    return jnp.concatenate(halves, 0)


def rates_kernel(
    masks_ref, rate_ref, heat_ref, rows_ref, cols_ref, react_ref,
    brate_ref, burn_ref, bheat_ref, table_ref, w1_ref, w2_ref, w3_ref, tab,
):
    tab[...] = jnp.zeros_like(tab)
    tab[0:13, 0:64] = rate_ref[...]
    tab[14:15, 0:64] = heat_ref[...]
    t = tab[...]
    t = t + pltpu.roll(t, 64, 1)
    row = lax.broadcasted_iota(jnp.int32, (16, 128), 0)
    h = jnp.concatenate(
        [jnp.where(row < 13, t, 0.0), jnp.where(row == 13, 1.0, 0.0), jnp.where(row == 14, t, 0.0)], 1
    )
    hi, lo = split(h)
    half = jnp.concatenate([hi.astype(F32), lo.astype(F32), jnp.zeros((32, 384), F32)], 0)
    low = (lanes((64, 384)) & 127) < 64
    table_ref[...] = jnp.concatenate([jnp.where(low, half, 0.0), jnp.where(low, 0.0, half)], 0).astype(BF)

    zero = jnp.zeros((C, C), F32)
    eye = jnp.where(lax.broadcasted_iota(jnp.int32, (C, C), 0) == lanes((C, C)), 1.0, 0.0)

    def both(m):
        return split(jnp.concatenate([jnp.concatenate([m, zero], 1), jnp.concatenate([zero, m], 1)], 0).T)

    r_hi, r_lo = both(rows_ref[...] + eye)
    c_hi, c_lo = both(cols_ref[...] + eye)
    e_hi, e_lo = both(react_ref[...])
    w1_ref[...] = jnp.concatenate([jnp.concatenate([r_hi, c_hi], 1)] * 2, 0)
    w2_ref[...] = jnp.concatenate([r_lo, c_lo], 1)
    w3_ref[...] = jnp.concatenate(
        [jnp.concatenate([e_hi, e_lo], 1), jnp.concatenate([e_hi, jnp.zeros((128, 128), BF)], 1)], 0
    )
    for k in range(OWN):
        put_rates(masks_ref, table_ref, HALO + k, k, 0, brate_ref, burn_ref, bheat_ref)


def put_rates(masks_ref, table_ref, r, k, start, brate_ref, burn_ref, bheat_ref):
    pick = lambda base: (masks_ref[base + r : base + r + 1], masks_ref[base + 63 - r : base + 64 - r])
    hot = onehot(pick(FUEL), pick(BURN), pick(LIT)).T.astype(BF)
    got = jnp.dot(hot, table_ref[...], preferred_element_type=F32)
    at = slice(start, start + COLS)
    brate_ref[k, at], burn_ref[k, at], bheat_ref[k, at] = got[:, 0:128], got[:, 128:256], got[:, 256:384]


def put_edge_rates(edge_ref, table_ref, r0, base_r, starts, brate_ref, burn_ref, bheat_ref):
    rows = []
    for base in (FUEL, BURN, LIT):
        halves = []
        for h in range(2):
            total = None
            for k in range(8):
                p = r0 + k if h == 0 else 63 - r0 - k
                part = edge_ref[base + p : base + p + 1]
                part = pltpu.roll(part, 16 * k, 1) if k else part
                total = part if total is None else total + part
            halves.append(total)
        rows.append(halves)
    got = jnp.dot(onehot(*rows).T.astype(BF), table_ref[...], preferred_element_type=F32)
    for k in range(8):
        for side, start in zip((0, 8), starts):
            part = got[16 * k + side : 16 * k + side + 8]
            r, at = r0 + k - base_r, slice(start, start + HALO)
            brate_ref[r, at], burn_ref[r, at], bheat_ref[r, at] = part[:, 0:128], part[:, 128:256], part[:, 256:384]


def rates(masks, rate, heat, rows, cols, react):
    cells = ((OWN, COLS, LANES), F32)
    return call(
        rates_kernel, "rates",
        [cells, cells, cells, ((128, 384), BF), ((256, 256), BF), ((128, 256), BF), ((256, 256), BF)],
        [((16, 128), F32)],
    )(masks, rate, heat, rows, cols, react)


def turned_edges(left_ref, right_ref, k):
    both = jnp.concatenate([left_ref[k], right_ref[k], jnp.zeros((112, 128), F32)], 0)
    return both.T


def rows_kernel(
    field_ref, masks_ref, near_ref, far_ref, table_ref,
    out_near_ref, out_far_ref, edge_ref, left_ref, right_ref, up_ref, down_ref,
):
    is_even = even("col")
    left_ref[...] = jnp.where(is_even, far_ref[...], near_ref[...])
    right_ref[...] = jnp.where(is_even, near_ref[...], far_ref[...])
    low = lanes((WIDTH, LANES)) < C

    def tile(k):
        return jnp.concatenate([left_ref[k], field_ref[k], right_ref[k]], 0)

    for t in range(4):
        near, far = tile(t), pltpu.roll(tile(4 + t), C, 1)
        at = slice(t * WIDTH, (t + 1) * WIDTH)
        up_ref[at] = jnp.where(low, near, far)
        down_ref[at] = jnp.where(low, far, near)
    edge_ref[0:128] = turned_edges(left_ref, right_ref, OWN)
    edge_ref[128:256] = turned_edges(left_ref, right_ref, OWN + 1)
    for i, base in enumerate((FUEL, BURN, LIT)):
        for ref, first in ((up_ref, HALO), (down_ref, HALO + ROWS - 8)):
            rows = slice(base + first, base + first + 8)
            ref[MSG + 8 * i : MSG + 8 * i + 8] = masks_ref[rows]
            ref[MSG + 24 + 8 * i : MSG + 32 + 8 * i] = edge_ref[rows]
    row_even = even("row")
    out_near_ref[...] = jnp.where(row_even, down_ref[...], up_ref[...])
    out_far_ref[...] = jnp.where(row_even, up_ref[...], down_ref[...])


def row_messages(field, masks, near, far, table):
    message = ((MSG + 48, LANES), F32)
    side = ((OWN + 2, HALO, LANES), F32)
    return call(
        rows_kernel, "rows", [message, message, ((256, LANES), F32), side, side], [message, message]
    )(field, masks, near, far, table)


class Stage:
    def __init__(self, first, last, second, load, old, store, rate, weights, S, W, T, group):
        self.first, self.last, self.second = first, last, second
        self.load, self.old, self.store, self.rate = load, old, store, rate
        self.weights, self.S, self.W, self.T, self.group = weights, S, W, T, group

    def mix(self, r, n, keep=None):
        w1, w2, w3 = self.weights
        brate, burn, bheat = self.rate
        x = jnp.concatenate([self.load(r + k) for k in range(n)], 0)
        hi, lo = split(x)
        t_hi, t_lo = split(jnp.tanh(x))
        sw = jnp.dot(jnp.concatenate([hi, lo], 1), w1[...], preferred_element_type=F32)
        sw = sw + jnp.dot(hi, w2[...], preferred_element_type=F32)
        tt = jnp.dot(jnp.concatenate([t_hi, t_lo], 1), w3[...], preferred_element_type=F32)
        tt = tt[:, 0:LANES] + tt[:, LANES:]
        for k in range(n):
            at = slice(k * WIDTH, (k + 1) * WIDTH)
            q = r + k
            rest = None
            self.S[q] = sw[at, 0:LANES]
            self.W[q, 8 : 8 + WIDTH] = sw[at, LANES:]
            if self.first <= q < self.last or keep:
                rest = 0.5 * x[at] + (burn(q) * tt[at] + bheat(q))
                self.T[q] = rest
            if q == TILES - 1:
                self.S[q + 1] = pltpu.roll(sw[at, 0:LANES], C, 1)
            if keep:
                keep(q, sw[at, 0:LANES], sw[at, LANES:], rest)

    def post(self, q, s_at, w_at, t_at):
        centre = s_at(q) + w_at(q, 8)
        around = (s_at(q - 1) + s_at(q + 1)) + (w_at(q, 7) + w_at(q, 9))
        g = t_at(q) + self.rate[0](q) * (around - centre - centre)
        self.store(q, 0.5 * (self.old(q) + g) if self.second else g)

    def run(self, end, s_at, w_at, t_at, keep=None):
        r, todo = self.first - 1, self.first
        while r < end:
            n = min(self.group, end - r)
            if 0 < end - r - n < 3:
                n = end - r
            self.mix(r, n, keep)
            r += n
            limit = self.last if r == end else min(self.last, r - 1)
            for q in range(todo, limit):
                self.post(q, s_at, w_at, t_at)
            todo = max(todo, limit)


def beside(side, own):
    return lambda r: jnp.concatenate([side[r - HALO, 0:8], own[r - HALO], side[r - HALO, 8:16]], 0)


def clear_margins(W):
    W[:, 0:8] = jnp.zeros((W.shape[0], 8, LANES), F32)
    W[:, 8 + WIDTH :] = jnp.zeros((W.shape[0], 8, LANES), F32)


def inner_kernel(
    field_ref, left_ref, right_ref, edge_ref, brate_in, burn_in, bheat_in, table_ref, w1, w2, w3,
    A, B, brate, burn, bheat, kept_s, kept_w, kept_t, S, W, T,
):
    clear_margins(W)
    clear_margins(kept_w)
    for r0 in range(HALO, TILES, 8):
        put_edge_rates(edge_ref, table_ref, r0, HALO, (0, 8), brate, burn, bheat)
    rate = [beside(brate, brate_in), beside(burn, burn_in), beside(bheat, bheat_in)]

    def start(r):
        k = r - HALO
        return jnp.concatenate([left_ref[k], field_ref[k], right_ref[k]], 0)

    A[HALO] = start(HALO)
    A[HALO + 1] = start(HALO + 1)
    for s in range(1, STAGES + 1):
        src, dst = (A, B) if s % 2 else (B, A)

        def store(q, value, dst=dst):
            dst[q] = value

        def keep(q, s_value, w_value, t_value, s=s):
            near = q - (HALO + s - 1)
            if near < 2:
                kept_s[s - 1, near] = s_value
            if near == 0:
                kept_w[s - 1, 8 : 8 + WIDTH] = w_value
                kept_t[s - 1] = t_value

        stage = Stage(
            HALO + s, TILES, s % 2 == 0,
            start if s == 1 else (lambda r, src=src: src[r]),
            start if s == 2 else (lambda r, dst=dst: dst[r]),
            store, rate, (w1, w2, w3), S, W, T, INNER_GROUP,
        )
        stage.run(TILES, lambda q: S[q], lambda q, o: W[q, o : o + WIDTH], lambda q: T[q], keep)


def inner(field, left, right, edge, rate_arrays):
    cells = ((TILES, WIDTH, LANES), F32)
    edges = ((OWN, 2 * HALO, LANES), F32)
    return call(
        inner_kernel, "inner",
        [cells, cells, edges, edges, edges, ((STAGES, 2, WIDTH, LANES), F32),
         ((STAGES, WIDTH + 16, LANES), F32), ((STAGES, WIDTH, LANES), F32)],
        [((TILES + 1, WIDTH, LANES), F32), ((TILES, WIDTH + 16, LANES), F32), cells],
    )(field, left, right, edge, *rate_arrays)


def outer_kernel(
    A_in, B_in, brate_side, burn_side, bheat_side, kept_s, kept_w, kept_t, brate_in, burn_in, bheat_in,
    near_ref, far_ref, table_ref, w1, w2, w3,
    out_ref, A, B, brate, burn, bheat, masks, edge, S, W, T,
):
    low = lanes((WIDTH, LANES)) < C
    row_even = even("row")

    def arrived(at):
        near, far = near_ref[at], far_ref[at]
        return jnp.where(row_even, far, near), jnp.where(row_even, near, far)

    for t in range(4):
        top, bottom = arrived(slice(t * WIDTH, (t + 1) * WIDTH))
        A[7 - t] = pltpu.roll(jnp.where(low, bottom, top), C, 1)
        A[3 - t] = jnp.where(low, top, bottom)
    clear_margins(W)
    for i, base in enumerate((FUEL, BURN, LIT)):
        for ref, offset in ((masks, MSG + 8 * i), (edge, MSG + 24 + 8 * i)):
            top, bottom = arrived(slice(offset, offset + 8))
            ref[base : base + 8] = top
            ref[base + HALO + ROWS : base + HEIGHT] = bottom
    for r in range(HALO):
        put_rates(masks, table_ref, r, r, HALO, brate, burn, bheat)
    put_edge_rates(edge, table_ref, 0, 0, (0, HALO + COLS), brate, burn, bheat)

    def reader(near, side, own):
        far = beside(side, own)
        return lambda r: near[r] if r < HALO else far(r)

    rate = [
        reader(brate, brate_side, brate_in), reader(burn, burn_side, burn_in), reader(bheat, bheat_side, bheat_in)
    ]
    for s in range(1, STAGES + 1):
        (src, dst), dst_in = ((A, B), B_in) if s % 2 else ((B, A), A_in)
        edge_tile = HALO + s - 1

        def store(q, value, dst=dst):
            dst[q] = value

        def old(q, dst=dst, dst_in=dst_in, s=s):
            return dst[q] if q < HALO + s - 2 else dst_in[q]

        def load(q, src=src):
            return src[q]

        def s_at(q, e=edge_tile, s=s):
            return S[q] if q < e else kept_s[s - 1, q - e]

        def w_at(q, o, e=edge_tile, s=s):
            return W[q, o : o + WIDTH] if q < e else kept_w[s - 1, o : o + WIDTH]

        def t_at(q, e=edge_tile, s=s):
            return T[q] if q < e else kept_t[s - 1]

        stage = Stage(
            s, HALO + s, s % 2 == 0, load, old, store, rate, (w1, w2, w3), S, W, T, OUTER_GROUP
        )
        stage.run(edge_tile, s_at, w_at, t_at)
    flat = out_ref.reshape(C * ROWS, COLS)
    for k in reversed(range(OWN)):
        r = HALO + k
        turned = (A if r < 2 * HALO else A_in)[r, HALO : HALO + COLS].T
        flat[pl.ds(k, C, stride=ROWS), :] = turned[0:C]
        flat[pl.ds(ROWS - 1 - k, C, stride=ROWS), :] = turned[C:]


def outer(states, rate_arrays, near, far):
    few = 2 * HALO
    cells = ((few, WIDTH, LANES), F32)
    edge_cells = ((HALO, WIDTH, LANES), F32)
    return call(
        outer_kernel, "outer", [((C, ROWS, COLS), F32)],
        [cells, cells, edge_cells, edge_cells, edge_cells, ((192, COLS), F32), ((192, COLS), F32),
         cells, ((few, WIDTH + 16, LANES), F32), cells],
    )(*states, *rate_arrays[:3], near, far, *rate_arrays[3:])[0]


def exchange(near, far, axis):
    size = lax.axis_size(axis)

    def swap(x, start):
        pairs = [(i, i + 1) for i in range(start, size - 1, 2)]
        return lax.ppermute(x, axis, pairs + [(b, a) for a, b in pairs])

    far = swap(far, 1)
    return swap(near, 0), far


def per_device(
    fire_state, fuel_class, firebreak, ignition,
    spread_rate, spread_rows, spread_cols, reaction, ignition_heat,
):
    field, masks, near, far = pack(fire_state, fuel_class, firebreak, ignition)
    near, far = exchange(near, far, "col")
    rate_arrays = rates(masks, spread_rate, ignition_heat[None], spread_rows, spread_cols, reaction)
    near, far, edge, left, right = row_messages(field, masks, near, far, rate_arrays[3])
    near, far = exchange(near, far, "row")
    states = inner(field, left, right, edge, rate_arrays)
    return outer(states, rate_arrays, near, far)


def solution(mesh):
    whole = P(None, "row", "col")
    cells = P("row", "col")
    return jax.shard_map(
        per_device,
        mesh=mesh,
        in_specs=(whole, cells, cells, cells, P(), P(), P(), P(), P()),
        out_specs=whole,
        check_vma=False,
    )
```

time: 47 us -> 39.5 us (0.84)
  the two profiles are of different devices: /device:TPU:15 before, /device:TPU:104 now
where the time goes in v3:
time: 39.5 us; the launch traced here: 39.2 us
  Pallas kernels  20.5 us (52%)
  starting transfers between devices  10 us (25%)
  waiting for transfers between devices  4.89 us (12%)
  local copies, waits for them, and re-layouts  3.64 us (9%)
    pallas_call x1, Pallas kernels, inner(): call(inner_kernel, 'inner', [cells, cells, edges, edges, edges, ((STAGES,...  11.9 us
    ppermute x4, starting transfers between devices, swap(): return lax.ppermute(x, axis, pairs + [(b, a) for a, b in pairs])  10 us
    pallas_call x1, Pallas kernels, outer(): call(outer_kernel, 'outer', [((C, ROWS, COLS), F32)], [cells, cells, edge...  6.54 us
    ppermute x4, waiting for transfers between devices, swap(): return lax.ppermute(x, axis, pairs + [(b, a) for a, b in pairs])  4.89 us
    unnamed x18, local copies, waits for them, and re-layouts  3.64 us
    pallas_call x1, Pallas kernels, pack(): call(pack_kernel, 'pack', [((OWN, COLS, LANES), F32), ((256, COLS), F32),...  1.06 us
    pallas_call x1, Pallas kernels, rates(): call(rates_kernel, 'rates', [cells, cells, cells, ((128, 384), BF), ((256...  0.86 us
  transfers between devices with their start and end apart: 4, of which 1 were waited for; matrix products, arithmetic and copies ran while one was open for 0% of the time, Pallas kernels for 32%

profile of v3, /device:TPU:104, one launch (start us, length us, event | category | flops | bytes accessed | tf_op | source)
XLA Modules:
  0.0 39.2 jit_solution(17337012792830585342)
XLA Ops:
  0.0 0.0 copy-start
  0.0 1.4 %copy-done = f32[64,48,128]{2,1,0:T(8,128)S(1)} copy-done((f32[64,48,128]{2,1,0:T(8,128)S(1)}, f32[64,48,128]{2,1,0:T(8,128)}, u32[]{:S(2)}) %copy-start) | copy-done | bytes 1572888
  1.4 0.0 copy-start.4
  1.4 0.7 %copy-done.4 = s32[48,128]{1,0:T(8,128)S(1)} copy-done((s32[48,128]{1,0:T(8,128)S(1)}, s32[48,128]{1,0:T(8,128)}, u32[]{:S(2)}) %copy-start.4) | copy-done | bytes 24600
  2.1 0.0 copy-start.5
  2.1 0.7 %copy-done.5 = s32[48,128]{1,0:T(8,128)S(1)} copy-done((s32[48,128]{1,0:T(8,128)S(1)}, s32[48,128]{1,0:T(8,128)}, u32[]{:S(2)}) %copy-start.5) | copy-done | bytes 24600
  2.9 0.0 copy-start.6
  2.9 0.7 %copy-done.6 = s32[48,128]{1,0:T(8,128)S(1)} copy-done((s32[48,128]{1,0:T(8,128)S(1)}, s32[48,128]{1,0:T(8,128)}, u32[]{:S(2)}) %copy-start.6) | copy-done | bytes 24600
  3.6 0.0 copy-start.1
  3.6 0.0 copy-start.2
  3.6 0.0 copy-start.3
  3.6 0.0 copy-start.7
  3.6 0.0 copy-start.8
  3.6 1.1 %pack.1 = (f32[24,128,128]{2,1,0:T(8,128)S(1)}, f32[256,128]{1,0:T(8,128)S(1)}, f32[26,8,128]{2,1,0:T(8,128)S(1)}, f32[26,8,128]{2,1,0:T(8,128)S(1)}) custom-call(f32[64,48,128]{2,1,0:T(8,128)S(1)} %copy-done, s32[48,128]{1,0:T(8,128)S(1)} %copy-done.4, s32[48,128]{1,0:T(8,128)S(1)} %copy-done.5, s32[48,128]{1,0:T(8,128)S(1)} %copy-done.6), custom_call_target="tpu_custom_call" | custom-call | tf_op jit(solution)/shard_map/pack/pallas_call | solution.py:96
  4.7 0.1 collective-permute-start
  4.8 4.7 %collective-permute-start.1 = (f32[26,8,128]{2,1,0:T(8,128)S(1)}, f32[26,8,128]{2,1,0:T(8,128)S(1)}, u32[]{:S(2)}, u32[]{:S(2)}) collective-permute-start(f32[26,8,128]{2,1,0:T(8,128)S(1)} %get-tuple-element.32), channel_id=1, source_target_pairs={{1,2},{3,4},{5,6},{7,8},{9,10},{11,12},{13,14},{2,1},{4,3},{6,5},{... | collective-permute-start | bytes 319496 | tf_op jit(solution)/shard_map/ppermute | solution.py:421
  9.6 0.0 copy-done.1
  9.6 0.0 copy-done.2
  9.6 0.0 copy-done.3
  9.6 0.0 copy-done.7
  9.6 0.0 copy-done.8
  9.6 0.9 %rates.1 = (f32[24,128,128]{2,1,0:T(8,128)S(1)}, f32[24,128,128]{2,1,0:T(8,128)S(1)}, f32[24,128,128]{2,1,0:T(8,128)S(1)}, bf16[128,384]{1,0:T(8,128)(2,1)S(1)},...) custom-call(f32[256,128]{1,0:T(8,128)S(1)} %get-tuple-element.30.masks_ref, ...), custom_call_target="tpu_custom_call" | custom-call | tf_op jit(solution)/shard_map/rates/pallas_call | solution.py:180
  10.5 0.0 collective-permute-done.near_ref
  10.5 4.9 %collective-permute-done.1.far_ref = f32[26,8,128]{2,1,0:T(8,128)S(1)} collective-permute-done((f32[26,8,128]{2,1,0:T(8,128)S(1)}, f32[26,8,128]{2,1,0:T(8,128)S(1)}, u32[]{:S(2)}, u32[]{:S(2)}) %collective-permute-start.1) | collective-permute-done | bytes 106528 | tf_op jit(solution)/shard_map/ppermute | solution.py:421
  15.4 0.2 rows.1
  15.6 0.7 %collective-permute-start.2 = (f32[624,128]{1,0:T(8,128)S(1)}, f32[624,128]{1,0:T(8,128)S(1)}, u32[]{:S(2)}, u32[]{:S(2)}) collective-permute-start(f32[624,128]{1,0:T(8,128)S(1)} %get-tuple-element.51), channel_id=1, source_target_pairs={{0,16},{32,48},{64,80},{96,112},{16,0},{48,32},{80,64},{112,96},{1... | collective-permute-start | bytes 958472 | tf_op jit(solution)/shard_map/ppermute | solution.py:421
  16.3 4.5 %collective-permute-start.3 = (f32[624,128]{1,0:T(8,128)S(1)}, f32[624,128]{1,0:T(8,128)S(1)}, u32[]{:S(2)}, u32[]{:S(2)}) collective-permute-start(f32[624,128]{1,0:T(8,128)S(1)} %get-tuple-element.52), channel_id=1, source_target_pairs={{16,32},{48,64},{80,96},{32,16},{64,48},{96,80},{17,33},{49,65},{8... | collective-permute-start | bytes 958472 | tf_op jit(solution)/shard_map/ppermute | solution.py:421
  20.8 11.9 %inner.1 = (f32[32,144,128]{2,1,0:T(8,128)S(1)}, f32[32,144,128]{2,1,0:T(8,128)S(1)}, f32[24,16,128]{2,1,0:T(8,128)S(1)}, f32[24,16,128]{2,1,0:T(8,128)S(1)}, f3...) custom-call(f32[24,128,128]{2,1,0:T(8,128)S(1)} %get-tuple-element.2, ...), custom_call_target="tpu_custom_call" | custom-call | tf_op jit(solution)/shard_map/inner/pallas_call | solution.py:330
  32.6 0.0 collective-permute-done.2.near_ref
  32.6 0.0 collective-permute-done.3.far_ref
  32.7 6.5 %outer.1 = f32[64,48,128]{2,1,0:T(8,128)} custom-call(f32[32,144,128]{2,1,0:T(8,128)S(1)} %get-tuple-element.43.A_in, f32[32,144,128]{2,1,0:T(8,128)S(1)} %get-tuple-element.44.B_in, f32[24,16,128]{2,1,0:T(8,128)S(1)} %get-tuple-element.45.brate_side, f32[24,16,128]{2,1,0:T(8,128)S(1)} %get-tuple-element.46.burn_side, ...), custom_call_target="tpu_custom_call" | custom-call | tf_op jit(solution)/shard_map/outer/pallas_call | solution.py:409
Async XLA Ops:
  0.0 1.4 %copy-start = (f32[64,48,128]{2,1,0:T(8,128)S(1)}, f32[64,48,128]{2,1,0:T(8,128)}, u32[]{:S(2)}) copy-start(f32[64,48,128]{2,1,0:T(8,128)} %x_hbm.1) | copy-start | bytes 4718596
  1.4 0.7 %copy-start.4 = (s32[48,128]{1,0:T(8,128)S(1)}, s32[48,128]{1,0:T(8,128)}, u32[]{:S(2)}) copy-start(s32[48,128]{1,0:T(8,128)} %fuel_hbm.1) | copy-start | bytes 73732
  2.1 0.7 %copy-start.5 = (s32[48,128]{1,0:T(8,128)S(1)}, s32[48,128]{1,0:T(8,128)}, u32[]{:S(2)}) copy-start(s32[48,128]{1,0:T(8,128)} %break_hbm.1) | copy-start | bytes 73732
  2.9 0.7 %copy-start.6 = (s32[48,128]{1,0:T(8,128)S(1)}, s32[48,128]{1,0:T(8,128)}, u32[]{:S(2)}) copy-start(s32[48,128]{1,0:T(8,128)} %lit_hbm.1) | copy-start | bytes 73732
  3.6 5.9 %copy-start.1 = (f32[64,64]{1,0:T(8,128)S(1)}, f32[64,64]{1,0:T(8,128)}, u32[]{:S(2)}) copy-start(f32[64,64]{1,0:T(8,128)} %rows_ref.1) | copy-start | bytes 49156
  3.6 5.9 %copy-start.2 = (f32[64,64]{1,0:T(8,128)S(1)}, f32[64,64]{1,0:T(8,128)}, u32[]{:S(2)}) copy-start(f32[64,64]{1,0:T(8,128)} %cols_ref.1) | copy-start | bytes 49156
  3.6 5.9 %copy-start.3 = (f32[64,64]{1,0:T(8,128)S(1)}, f32[64,64]{1,0:T(8,128)}, u32[]{:S(2)}) copy-start(f32[64,64]{1,0:T(8,128)} %react_ref.1) | copy-start | bytes 49156
  3.6 6.0 %copy-start.7 = (f32[13,64]{1,0:T(8,128)S(1)}, f32[13,64]{1,0:T(8,128)}, u32[]{:S(2)}) copy-start(f32[13,64]{1,0:T(8,128)} %rate_ref.1) | copy-start | bytes 9988
  3.6 6.0 %copy-start.8 = (f32[64]{0:T(128)S(1)}, f32[64]{0:T(128)}, u32[]{:S(2)}) copy-start(f32[64]{0:T(128)} %param.17) | copy-start | bytes 772
  4.7 5.8 %collective-permute-start = (f32[26,8,128]{2,1,0:T(8,128)S(1)}, f32[26,8,128]{2,1,0:T(8,128)S(1)}, u32[]{:S(2)}, u32[]{:S(2)}) collective-permute-start(f32[26,8,128]{2,1,0:T(8,128)S(1)} %get-tuple-element.31), channel_id=1, source_target_pairs={{0,1},{2,3},{4,5},{6,7},{8,9},{10,11},{12,13},{14,15},{1,0},{3,2},... | collective-permute-start | bytes 319496 | tf_op jit(solution)/shard_map/ppermute | solution.py:421
  4.8 10.6 %collective-permute-start.1 = (f32[26,8,128]{2,1,0:T(8,128)S(1)}, f32[26,8,128]{2,1,0:T(8,128)S(1)}, u32[]{:S(2)}, u32[]{:S(2)}) collective-permute-start(f32[26,8,128]{2,1,0:T(8,128)S(1)} %get-tuple-element.32), channel_id=1, source_target_pairs={{1,2},{3,4},{5,6},{7,8},{9,10},{11,12},{13,14},{2,1},{4,3},{6,5},{... | collective-permute-start | bytes 319496 | tf_op jit(solution)/shard_map/ppermute | solution.py:421
  15.6 17.1 %collective-permute-start.2 = (f32[624,128]{1,0:T(8,128)S(1)}, f32[624,128]{1,0:T(8,128)S(1)}, u32[]{:S(2)}, u32[]{:S(2)}) collective-permute-start(f32[624,128]{1,0:T(8,128)S(1)} %get-tuple-element.51), channel_id=1, source_target_pairs={{0,16},{32,48},{64,80},{96,112},{16,0},{48,32},{80,64},{112,96},{1... | collective-permute-start | bytes 958472 | tf_op jit(solution)/shard_map/ppermute | solution.py:421
  16.3 16.4 %collective-permute-start.3 = (f32[624,128]{1,0:T(8,128)S(1)}, f32[624,128]{1,0:T(8,128)S(1)}, u32[]{:S(2)}, u32[]{:S(2)}) collective-permute-start(f32[624,128]{1,0:T(8,128)S(1)} %get-tuple-element.52), channel_id=1, source_target_pairs={{16,32},{48,64},{80,96},{32,16},{64,48},{96,80},{17,33},{49,65},{8... | collective-permute-start | bytes 958472 | tf_op jit(solution)/shard_map/ppermute | solution.py:421

commit v4 on v3

--- a/solution.py
+++ b/solution.py
@@ -97,7 +97,7 @@
         pack_kernel, "pack", [((OWN, COLS, LANES), F32), ((256, COLS), F32), message, message],
         [((C, ROWS, COLS), F32)], from_hbm=4,
         extra=[pltpu.VMEM((3, ROWS, COLS), jnp.int32), pltpu.SemaphoreType.DMA((9,))],
-    )(x, fuel, firebreak, lit)
+    )(*[pltpu.with_memory_space_constraint(a, pltpu.HBM) for a in (x, fuel, firebreak, lit)])
 
 
 def onehot(fuel, burn, lit):

time: 39.5 us -> 36.6 us (0.927)
  local copies, waits for them, and re-layouts: 3.64 us -> 0.02 us
  Pallas kernels: 20.5 us -> 21.4 us
    unnamed x18 -> x10, local copies, waits for them, and re-layouts: 3.64 us -> 0.02 us
    pallas_call x1, Pallas kernels: 1.06 us -> 1.92 us  [pack(): call(pack_kernel, 'pack', [((OWN, COLS, LANES), F32), ((256, COLS), F32),...]
  transfers between devices with their start and end apart: 4 -> 4, of which waited for: 1 -> 1; matrix products, arithmetic and copies ran while one was open for 0% -> 0% of each run, Pallas kernels for 32% -> 35%
where the time goes in v4:
time: 36.6 us; the launch traced here: 36.4 us
  Pallas kernels  21.4 us (58%)
  starting transfers between devices  10 us (27%)
  waiting for transfers between devices  4.89 us (13%)
    pallas_call x1, Pallas kernels, inner(): call(inner_kernel, 'inner', [cells, cells, edges, edges, edges, ((STAGES,...  11.8 us
    ppermute x4, starting transfers between devices, swap(): return lax.ppermute(x, axis, pairs + [(b, a) for a, b in pairs])  10 us
    pallas_call x1, Pallas kernels, outer(): call(outer_kernel, 'outer', [((C, ROWS, COLS), F32)], [cells, cells, edge...  6.53 us
    ppermute x4, waiting for transfers between devices, swap(): return lax.ppermute(x, axis, pairs + [(b, a) for a, b in pairs])  4.89 us
    pallas_call x1, Pallas kernels, pack(): call(pack_kernel, 'pack', [((OWN, COLS, LANES), F32), ((256, COLS), F32),...  1.92 us
    pallas_call x1, Pallas kernels, rates(): call(rates_kernel, 'rates', [cells, cells, cells, ((128, 384), BF), ((256...  0.86 us
  transfers between devices with their start and end apart: 4, of which 1 were waited for; matrix products, arithmetic and copies ran while one was open for 0% of the time, Pallas kernels for 35%

profile of v4, /device:TPU:104, one launch (start us, length us, event | category | flops | bytes accessed | tf_op | source)
XLA Modules:
  0.0 36.4 jit_solution(4822221598612634277)
XLA Ops:
  0.0 0.0 copy-start.4
  0.0 0.0 copy-start.2
  0.0 0.0 copy-start.1
  0.0 0.0 copy-start
  0.0 0.0 copy-start.3
  0.0 1.9 %pack.1 = (f32[24,128,128]{2,1,0:T(8,128)S(1)}, f32[256,128]{1,0:T(8,128)S(1)}, f32[26,8,128]{2,1,0:T(8,128)S(1)}, f32[26,8,128]{2,1,0:T(8,128)S(1)}) custom-call(f32[64,48,128]{2,1,0:T(8,128)} %x_hbm.1, s32[48,128]{1,0:T(8,128)} %fuel_hbm.1, s32[48,128]{1,0:T(8,128)} %break_hbm.1, s32[48,128]{1,0:T(8,128)} %lit_hbm.1), custom_call_target="tpu_custom_call" | custom-call | tf_op jit(solution)/shard_map/pack/pallas_call | solution.py:96
  2.0 0.1 collective-permute-start
  2.0 4.7 %collective-permute-start.1 = (f32[26,8,128]{2,1,0:T(8,128)S(1)}, f32[26,8,128]{2,1,0:T(8,128)S(1)}, u32[]{:S(2)}, u32[]{:S(2)}) collective-permute-start(f32[26,8,128]{2,1,0:T(8,128)S(1)} %get-tuple-element.32), channel_id=1, source_target_pairs={{1,2},{3,4},{5,6},{7,8},{9,10},{11,12},{13,14},{2,1},{4,3},{6,5},{... | collective-permute-start | bytes 319496 | tf_op jit(solution)/shard_map/ppermute | solution.py:421
  6.8 0.0 copy-done.4
  6.8 0.0 copy-done.2
  6.8 0.0 copy-done.1
  6.8 0.0 copy-done
  6.8 0.0 copy-done.3
  6.9 0.9 %rates.1 = (f32[24,128,128]{2,1,0:T(8,128)S(1)}, f32[24,128,128]{2,1,0:T(8,128)S(1)}, f32[24,128,128]{2,1,0:T(8,128)S(1)}, bf16[128,384]{1,0:T(8,128)(2,1)S(1)},...) custom-call(f32[256,128]{1,0:T(8,128)S(1)} %get-tuple-element.30.masks_ref, ...), custom_call_target="tpu_custom_call" | custom-call | tf_op jit(solution)/shard_map/rates/pallas_call | solution.py:180
  7.7 0.0 collective-permute-done.near_ref
  7.7 4.9 %collective-permute-done.1.far_ref = f32[26,8,128]{2,1,0:T(8,128)S(1)} collective-permute-done((f32[26,8,128]{2,1,0:T(8,128)S(1)}, f32[26,8,128]{2,1,0:T(8,128)S(1)}, u32[]{:S(2)}, u32[]{:S(2)}) %collective-permute-start.1) | collective-permute-done | bytes 106528 | tf_op jit(solution)/shard_map/ppermute | solution.py:421
  12.6 0.2 rows.1
  12.8 0.7 %collective-permute-start.2 = (f32[624,128]{1,0:T(8,128)S(1)}, f32[624,128]{1,0:T(8,128)S(1)}, u32[]{:S(2)}, u32[]{:S(2)}) collective-permute-start(f32[624,128]{1,0:T(8,128)S(1)} %get-tuple-element.51), channel_id=1, source_target_pairs={{0,16},{32,48},{64,80},{96,112},{16,0},{48,32},{80,64},{112,96},{1... | collective-permute-start | bytes 958472 | tf_op jit(solution)/shard_map/ppermute | solution.py:421
  13.5 4.5 %collective-permute-start.3 = (f32[624,128]{1,0:T(8,128)S(1)}, f32[624,128]{1,0:T(8,128)S(1)}, u32[]{:S(2)}, u32[]{:S(2)}) collective-permute-start(f32[624,128]{1,0:T(8,128)S(1)} %get-tuple-element.52), channel_id=1, source_target_pairs={{16,32},{48,64},{80,96},{32,16},{64,48},{96,80},{17,33},{49,65},{8... | collective-permute-start | bytes 958472 | tf_op jit(solution)/shard_map/ppermute | solution.py:421
  18.0 11.8 %inner.1 = (f32[32,144,128]{2,1,0:T(8,128)S(1)}, f32[32,144,128]{2,1,0:T(8,128)S(1)}, f32[24,16,128]{2,1,0:T(8,128)S(1)}, f32[24,16,128]{2,1,0:T(8,128)S(1)}, f3...) custom-call(f32[24,128,128]{2,1,0:T(8,128)S(1)} %get-tuple-element.2, ...), custom_call_target="tpu_custom_call" | custom-call | tf_op jit(solution)/shard_map/inner/pallas_call | solution.py:330
  29.9 0.0 collective-permute-done.2.near_ref
  29.9 0.0 collective-permute-done.3.far_ref
  29.9 6.5 %outer.1 = f32[64,48,128]{2,1,0:T(8,128)} custom-call(f32[32,144,128]{2,1,0:T(8,128)S(1)} %get-tuple-element.43.A_in, f32[32,144,128]{2,1,0:T(8,128)S(1)} %get-tuple-element.44.B_in, f32[24,16,128]{2,1,0:T(8,128)S(1)} %get-tuple-element.45.brate_side, f32[24,16,128]{2,1,0:T(8,128)S(1)} %get-tuple-element.46.burn_side, ...), custom_call_target="tpu_custom_call" | custom-call | tf_op jit(solution)/shard_map/outer/pallas_call | solution.py:409
Async XLA Ops:
  0.0 6.8 %copy-start.4 = (f32[64]{0:T(128)S(1)}, f32[64]{0:T(128)}, u32[]{:S(2)}) copy-start(f32[64]{0:T(128)} %param.17) | copy-start | bytes 772
  0.0 6.8 %copy-start.2 = (f32[64,64]{1,0:T(8,128)S(1)}, f32[64,64]{1,0:T(8,128)}, u32[]{:S(2)}) copy-start(f32[64,64]{1,0:T(8,128)} %react_ref.1) | copy-start | bytes 49156
  0.0 6.8 %copy-start.1 = (f32[64,64]{1,0:T(8,128)S(1)}, f32[64,64]{1,0:T(8,128)}, u32[]{:S(2)}) copy-start(f32[64,64]{1,0:T(8,128)} %cols_ref.1) | copy-start | bytes 49156
  0.0 6.8 %copy-start = (f32[64,64]{1,0:T(8,128)S(1)}, f32[64,64]{1,0:T(8,128)}, u32[]{:S(2)}) copy-start(f32[64,64]{1,0:T(8,128)} %rows_ref.1) | copy-start | bytes 49156
  0.0 6.8 %copy-start.3 = (f32[13,64]{1,0:T(8,128)S(1)}, f32[13,64]{1,0:T(8,128)}, u32[]{:S(2)}) copy-start(f32[13,64]{1,0:T(8,128)} %rate_ref.1) | copy-start | bytes 9988
  2.0 5.8 %collective-permute-start = (f32[26,8,128]{2,1,0:T(8,128)S(1)}, f32[26,8,128]{2,1,0:T(8,128)S(1)}, u32[]{:S(2)}, u32[]{:S(2)}) collective-permute-start(f32[26,8,128]{2,1,0:T(8,128)S(1)} %get-tuple-element.31), channel_id=1, source_target_pairs={{0,1},{2,3},{4,5},{6,7},{8,9},{10,11},{12,13},{14,15},{1,0},{3,2},... | collective-permute-start | bytes 319496 | tf_op jit(solution)/shard_map/ppermute | solution.py:421
  2.0 10.6 %collective-permute-start.1 = (f32[26,8,128]{2,1,0:T(8,128)S(1)}, f32[26,8,128]{2,1,0:T(8,128)S(1)}, u32[]{:S(2)}, u32[]{:S(2)}) collective-permute-start(f32[26,8,128]{2,1,0:T(8,128)S(1)} %get-tuple-element.32), channel_id=1, source_target_pairs={{1,2},{3,4},{5,6},{7,8},{9,10},{11,12},{13,14},{2,1},{4,3},{6,5},{... | collective-permute-start | bytes 319496 | tf_op jit(solution)/shard_map/ppermute | solution.py:421
  12.8 17.1 %collective-permute-start.2 = (f32[624,128]{1,0:T(8,128)S(1)}, f32[624,128]{1,0:T(8,128)S(1)}, u32[]{:S(2)}, u32[]{:S(2)}) collective-permute-start(f32[624,128]{1,0:T(8,128)S(1)} %get-tuple-element.51), channel_id=1, source_target_pairs={{0,16},{32,48},{64,80},{96,112},{16,0},{48,32},{80,64},{112,96},{1... | collective-permute-start | bytes 958472 | tf_op jit(solution)/shard_map/ppermute | solution.py:421
  13.5 16.4 %collective-permute-start.3 = (f32[624,128]{1,0:T(8,128)S(1)}, f32[624,128]{1,0:T(8,128)S(1)}, u32[]{:S(2)}, u32[]{:S(2)}) collective-permute-start(f32[624,128]{1,0:T(8,128)S(1)} %get-tuple-element.52), channel_id=1, source_target_pairs={{16,32},{48,64},{80,96},{32,16},{64,48},{96,80},{17,33},{49,65},{8... | collective-permute-start | bytes 958472 | tf_op jit(solution)/shard_map/ppermute | solution.py:421

commit v5 on v4

--- a/solution.py
+++ b/solution.py
@@ -111,8 +111,8 @@
 
 
 def rates_kernel(
-    masks_ref, rate_ref, heat_ref, rows_ref, cols_ref, react_ref,
-    brate_ref, burn_ref, bheat_ref, table_ref, w1_ref, w2_ref, w3_ref, tab,
+    masks_ref, rate_ref, heat_ref, rows_ref, cols_ref, react_ref, field_ref,
+    brate_ref, burn_ref, bheat_ref, table_ref, w1_ref, w2_ref, w3_ref, s_ref, w_ref, t_ref, tab,
 ):
     tab[...] = jnp.zeros_like(tab)
     tab[0:13, 0:64] = rate_ref[...]
@@ -144,6 +144,23 @@
     )
     for k in range(OWN):
         put_rates(masks_ref, table_ref, HALO + k, k, 0, brate_ref, burn_ref, bheat_ref)
+    for k0 in range(0, OWN, INNER_GROUP):
+        x = field_ref[k0 : k0 + INNER_GROUP].reshape(INNER_GROUP * COLS, LANES)
+        s_all, w_all, tt = mixed(x, (w1_ref, w2_ref, w3_ref))
+        for i in range(INNER_GROUP):
+            k, at = k0 + i, slice(i * COLS, (i + 1) * COLS)
+            s_ref[k], w_ref[k] = s_all[at], w_all[at]
+            t_ref[k] = 0.5 * x[at] + (burn_ref[k] * tt[at] + bheat_ref[k])
+
+
+def mixed(x, weights):
+    w1, w2, w3 = weights
+    hi, lo = split(x)
+    t_hi, t_lo = split(jnp.tanh(x))
+    sw = jnp.dot(jnp.concatenate([hi, lo], 1), w1[...], preferred_element_type=F32)
+    sw = sw + jnp.dot(hi, w2[...], preferred_element_type=F32)
+    tt = jnp.dot(jnp.concatenate([t_hi, t_lo], 1), w3[...], preferred_element_type=F32)
+    return sw[:, 0:LANES], sw[:, LANES:], tt[:, 0:LANES] + tt[:, LANES:]
 
 
 def put_rates(masks_ref, table_ref, r, k, start, brate_ref, burn_ref, bheat_ref):
@@ -175,13 +192,14 @@
             brate_ref[r, at], burn_ref[r, at], bheat_ref[r, at] = part[:, 0:128], part[:, 128:256], part[:, 256:384]
 
 
-def rates(masks, rate, heat, rows, cols, react):
+def rates(masks, rate, heat, rows, cols, react, field):
     cells = ((OWN, COLS, LANES), F32)
     return call(
         rates_kernel, "rates",
-        [cells, cells, cells, ((128, 384), BF), ((256, 256), BF), ((128, 256), BF), ((256, 256), BF)],
+        [cells, cells, cells, ((128, 384), BF), ((256, 256), BF), ((128, 256), BF), ((256, 256), BF),
+         cells, cells, cells],
         [((16, 128), F32)],
-    )(masks, rate, heat, rows, cols, react)
+    )(masks, rate, heat, rows, cols, react, field)
 
 
 def turned_edges(left_ref, right_ref, k):
@@ -233,28 +251,22 @@
         self.weights, self.S, self.W, self.T, self.group = weights, S, W, T, group
 
     def mix(self, r, n, keep=None):
-        w1, w2, w3 = self.weights
         brate, burn, bheat = self.rate
         x = jnp.concatenate([self.load(r + k) for k in range(n)], 0)
-        hi, lo = split(x)
-        t_hi, t_lo = split(jnp.tanh(x))
-        sw = jnp.dot(jnp.concatenate([hi, lo], 1), w1[...], preferred_element_type=F32)
-        sw = sw + jnp.dot(hi, w2[...], preferred_element_type=F32)
-        tt = jnp.dot(jnp.concatenate([t_hi, t_lo], 1), w3[...], preferred_element_type=F32)
-        tt = tt[:, 0:LANES] + tt[:, LANES:]
+        s_all, w_all, tt = mixed(x, self.weights)
         for k in range(n):
             at = slice(k * WIDTH, (k + 1) * WIDTH)
             q = r + k
             rest = None
-            self.S[q] = sw[at, 0:LANES]
-            self.W[q, 8 : 8 + WIDTH] = sw[at, LANES:]
+            self.S[q] = s_all[at]
+            self.W[q, 8 : 8 + WIDTH] = w_all[at]
             if self.first <= q < self.last or keep:
                 rest = 0.5 * x[at] + (burn(q) * tt[at] + bheat(q))
                 self.T[q] = rest
             if q == TILES - 1:
-                self.S[q + 1] = pltpu.roll(sw[at, 0:LANES], C, 1)
+                self.S[q + 1] = pltpu.roll(s_all[at], C, 1)
             if keep:
-                keep(q, sw[at, 0:LANES], sw[at, LANES:], rest)
+                keep(q, s_all[at], w_all[at], rest)
 
     def post(self, q, s_at, w_at, t_at):
         centre = s_at(q) + w_at(q, 8)
@@ -262,12 +274,14 @@
         g = t_at(q) + self.rate[0](q) * (around - centre - centre)
         self.store(q, 0.5 * (self.old(q) + g) if self.second else g)
 
-    def run(self, end, s_at, w_at, t_at, keep=None):
+    def run(self, end, s_at, w_at, t_at, keep=None, before=None):
         r, todo = self.first - 1, self.first
         while r < end:
             n = min(self.group, end - r)
             if 0 < end - r - n < 3:
                 n = end - r
+            if before:
+                before(r + n)
             self.mix(r, n, keep)
             r += n
             limit = self.last if r == end else min(self.last, r - 1)
@@ -287,9 +301,10 @@
 
 def inner_kernel(
     field_ref, left_ref, right_ref, edge_ref, brate_in, burn_in, bheat_in, table_ref, w1, w2, w3,
-    A, B, brate, burn, bheat, kept_s, kept_w, kept_t, S, W, T,
+    s_in, w_in, t_in, A, B, brate, burn, bheat, kept_s, kept_w, kept_t, S, W, T, side_s, side_t, W1,
 ):
     clear_margins(W)
+    clear_margins(W1)
     clear_margins(kept_w)
     for r0 in range(HALO, TILES, 8):
         put_edge_rates(edge_ref, table_ref, r0, HALO, (0, 8), brate, burn, bheat)
@@ -298,6 +313,26 @@
     def start(r):
         k = r - HALO
         return jnp.concatenate([left_ref[k], field_ref[k], right_ref[k]], 0)
+
+    x = jnp.concatenate([ref[k] for k in range(OWN) for ref in (left_ref, right_ref)], 0)
+    s_all, w_all, tt = mixed(x, (w1, w2, w3))
+    for k in range(OWN):
+        r, span = HALO + k, slice(16 * k, 16 * k + 16)
+        side_s[k] = s_all[span]
+        side_t[k] = 0.5 * x[span] + (burn[k] * tt[span] + bheat[k])
+        W1[r, 8:16] = w_all[span][0:8]
+        W1[r, 16 + COLS : 24 + COLS] = w_all[span][8:16]
+
+    def first_w(k):
+        W1[HALO + k, 16 : 16 + COLS] = w_in[k]
+
+    s_of, t_first = beside(side_s, s_in), beside(side_t, t_in)
+
+    def s_first(q):
+        return s_of(q) if q < TILES else pltpu.roll(s_of(TILES - 1), C, 1)
+
+    def w_first(q, o):
+        return W1[q, o : o + WIDTH]
 
     A[HALO] = start(HALO)
     A[HALO + 1] = start(HALO + 1)
@@ -317,11 +352,26 @@
 
         stage = Stage(
             HALO + s, TILES, s % 2 == 0,
-            start if s == 1 else (lambda r, src=src: src[r]),
+            lambda r, src=src: src[r],
             start if s == 2 else (lambda r, dst=dst: dst[r]),
             store, rate, (w1, w2, w3), S, W, T, INNER_GROUP,
         )
-        stage.run(TILES, lambda q: S[q], lambda q, o: W[q, o : o + WIDTH], lambda q: T[q], keep)
+        readers = (lambda q: S[q], lambda q, o: W[q, o : o + WIDTH], lambda q: T[q])
+        if s == 1:
+            first_w(0)
+            first_w(1)
+            for q in (HALO, HALO + 1):
+                keep(q, s_first(q), W1[q, 8 : 8 + WIDTH], t_first(q))
+            opening, finished = stage, [HALO + 1]
+            continue
+
+        def before(end):
+            for q in range(finished[0], end):
+                first_w(q - HALO)
+                opening.post(q, s_first, w_first, t_first)
+            finished[0] = max(finished[0], end)
+
+        stage.run(TILES, *readers, keep, before if s == 2 else None)
 
 
 def inner(field, left, right, edge, rate_arrays):
@@ -331,7 +381,8 @@
         inner_kernel, "inner",
         [cells, cells, edges, edges, edges, ((STAGES, 2, WIDTH, LANES), F32),
          ((STAGES, WIDTH + 16, LANES), F32), ((STAGES, WIDTH, LANES), F32)],
-        [((TILES + 1, WIDTH, LANES), F32), ((TILES, WIDTH + 16, LANES), F32), cells],
+        [((TILES + 1, WIDTH, LANES), F32), ((TILES, WIDTH + 16, LANES), F32), cells, edges, edges,
+         ((TILES, WIDTH + 16, LANES), F32)], limit=20,
     )(field, left, right, edge, *rate_arrays)
 
 
@@ -410,7 +461,7 @@
         outer_kernel, "outer", [((C, ROWS, COLS), F32)],
         [cells, cells, edge_cells, edge_cells, edge_cells, ((192, COLS), F32), ((192, COLS), F32),
          cells, ((few, WIDTH + 16, LANES), F32), cells],
-    )(*states, *rate_arrays[:3], near, far, *rate_arrays[3:])[0]
+    )(*states, *rate_arrays[:3], near, far, *rate_arrays[3:7])[0]
 
 
 def exchange(near, far, axis):
@@ -430,7 +481,9 @@
 ):
     field, masks, near, far = pack(fire_state, fuel_class, firebreak, ignition)
     near, far = exchange(near, far, "col")
-    rate_arrays = rates(masks, spread_rate, ignition_heat[None], spread_rows, spread_cols, reaction)
+    rate_arrays = rates(
+        masks, spread_rate, ignition_heat[None], spread_rows, spread_cols, reaction, field
+    )
     near, far, edge, left, right = row_messages(field, masks, near, far, rate_arrays[3])
     near, far = exchange(near, far, "row")
     states = inner(field, left, right, edge, rate_arrays)

time: 36.6 us -> 34.8 us (0.951)
  waiting for transfers between devices: 4.89 us -> 2.83 us
    ppermute x4, waiting for transfers between devices: 4.89 us -> 2.83 us  [swap(): return lax.ppermute(x, axis, pairs + [(b, a) for a, b in pairs])]
    pallas_call x1, Pallas kernels: 0.86 us -> 2.11 us  [rates(): call(rates_kernel, 'rates', [cells, cells, cells, ((128, 384), BF), ((256...]
    pallas_call x1, Pallas kernels: 11.8 us -> 10.7 us  [inner(): call(inner_kernel, 'inner', [cells, cells, edges, edges, edges, ((STAGES,...]
  transfers between devices with their start and end apart: 4 -> 4, of which waited for: 1 -> 1; matrix products, arithmetic and copies ran while one was open for 0% -> 0% of each run, Pallas kernels for 35% -> 37%
where the time goes in v5:
time: 34.8 us; the launch traced here: 34.5 us
  Pallas kernels  21.5 us (62%)
  starting transfers between devices  10 us (29%)
  waiting for transfers between devices  2.83 us (8%)
    pallas_call x1, Pallas kernels, inner(): call(inner_kernel, 'inner', [cells, cells, edges, edges, edges, ((STAGES,...  10.7 us
    ppermute x4, starting transfers between devices, swap(): return lax.ppermute(x, axis, pairs + [(b, a) for a, b in pairs])  10 us
    pallas_call x1, Pallas kernels, outer(): call(outer_kernel, 'outer', [((C, ROWS, COLS), F32)], [cells, cells, edge...  6.57 us
    ppermute x4, waiting for transfers between devices, swap(): return lax.ppermute(x, axis, pairs + [(b, a) for a, b in pairs])  2.83 us
    pallas_call x1, Pallas kernels, rates(): call(rates_kernel, 'rates', [cells, cells, cells, ((128, 384), BF), ((256...  2.11 us
    pallas_call x1, Pallas kernels, pack(): call(pack_kernel, 'pack', [((OWN, COLS, LANES), F32), ((256, COLS), F32),...  1.92 us
  transfers between devices with their start and end apart: 4, of which 1 were waited for; matrix products, arithmetic and copies ran while one was open for 0% of the time, Pallas kernels for 37%

profile of v5, /device:TPU:104, one launch (start us, length us, event | category | flops | bytes accessed | tf_op | source)
XLA Modules:
  0.0 34.5 jit_solution(15898689293926953656)
XLA Ops:
  0.0 0.0 copy-start.4
  0.0 0.0 copy-start.2
  0.0 0.0 copy-start.1
  0.0 0.0 copy-start
  0.0 0.0 copy-start.3
  0.0 1.9 %pack.1 = (f32[24,128,128]{2,1,0:T(8,128)S(1)}, f32[256,128]{1,0:T(8,128)S(1)}, f32[26,8,128]{2,1,0:T(8,128)S(1)}, f32[26,8,128]{2,1,0:T(8,128)S(1)}) custom-call(f32[64,48,128]{2,1,0:T(8,128)} %x_hbm.1, s32[48,128]{1,0:T(8,128)} %fuel_hbm.1, s32[48,128]{1,0:T(8,128)} %break_hbm.1, s32[48,128]{1,0:T(8,128)} %lit_hbm.1), custom_call_target="tpu_custom_call" | custom-call | tf_op jit(solution)/shard_map/pack/pallas_call | solution.py:96
  2.0 0.1 collective-permute-start
  2.0 4.7 %collective-permute-start.1 = (f32[26,8,128]{2,1,0:T(8,128)S(1)}, f32[26,8,128]{2,1,0:T(8,128)S(1)}, u32[]{:S(2)}, u32[]{:S(2)}) collective-permute-start(f32[26,8,128]{2,1,0:T(8,128)S(1)} %get-tuple-element.35), channel_id=1, source_target_pairs={{1,2},{3,4},{5,6},{7,8},{9,10},{11,12},{13,14},{2,1},{4,3},{6,5},{... | collective-permute-start | bytes 319496 | tf_op jit(solution)/shard_map/ppermute | solution.py:472
  6.8 0.0 copy-done.4
  6.8 0.0 copy-done.2
  6.8 0.0 copy-done.1
  6.8 0.0 copy-done
  6.8 0.0 copy-done.3
  6.9 2.1 %rates.1 = (f32[24,128,128]{2,1,0:T(8,128)S(1)}, f32[24,128,128]{2,1,0:T(8,128)S(1)}, f32[24,128,128]{2,1,0:T(8,128)S(1)}, bf16[128,384]{1,0:T(8,128)(2,1)S(1)},...) custom-call(f32[256,128]{1,0:T(8,128)S(1)} %get-tuple-element.33.mas, ...), custom_call_target="tpu_custom_call" | custom-call | tf_op jit(solution)/shard_map/rates/pallas_call | solution.py:197
  9.0 0.0 collective-permute-done.near_ref
  9.0 2.8 %collective-permute-done.1.far_ref = f32[26,8,128]{2,1,0:T(8,128)S(1)} collective-permute-done((f32[26,8,128]{2,1,0:T(8,128)S(1)}, f32[26,8,128]{2,1,0:T(8,128)S(1)}, u32[]{:S(2)}, u32[]{:S(2)}) %collective-permute-start.1) | collective-permute-done | bytes 106528 | tf_op jit(solution)/shard_map/ppermute | solution.py:472
  11.8 0.2 rows.1
  12.0 0.9 %collective-permute-start.2 = (f32[624,128]{1,0:T(8,128)S(1)}, f32[624,128]{1,0:T(8,128)S(1)}, u32[]{:S(2)}, u32[]{:S(2)}) collective-permute-start(f32[624,128]{1,0:T(8,128)S(1)} %get-tuple-element.57), channel_id=1, source_target_pairs={{0,16},{32,48},{64,80},{96,112},{16,0},{48,32},{80,64},{112,96},{1... | collective-permute-start | bytes 958472 | tf_op jit(solution)/shard_map/ppermute | solution.py:472
  12.9 4.3 %collective-permute-start.3 = (f32[624,128]{1,0:T(8,128)S(1)}, f32[624,128]{1,0:T(8,128)S(1)}, u32[]{:S(2)}, u32[]{:S(2)}) collective-permute-start(f32[624,128]{1,0:T(8,128)S(1)} %get-tuple-element.58), channel_id=1, source_target_pairs={{16,32},{48,64},{80,96},{32,16},{64,48},{96,80},{17,33},{49,65},{8... | collective-permute-start | bytes 958472 | tf_op jit(solution)/shard_map/ppermute | solution.py:472
  17.2 10.7 %inner.1 = (f32[32,144,128]{2,1,0:T(8,128)S(1)}, f32[32,144,128]{2,1,0:T(8,128)S(1)}, f32[24,16,128]{2,1,0:T(8,128)S(1)}, f32[24,16,128]{2,1,0:T(8,128)S(1)}, f3...) custom-call(f32[24,128,128]{2,1,0:T(8,128)S(1)} %get-tuple-element.3, ...), custom_call_target="tpu_custom_call" | custom-call | tf_op jit(solution)/shard_map/inner/pallas_call | solution.py:380
  27.9 0.0 collective-permute-done.2.near_ref
  28.0 0.0 collective-permute-done.3.far_ref
  28.0 6.6 %outer.1 = f32[64,48,128]{2,1,0:T(8,128)} custom-call(f32[32,144,128]{2,1,0:T(8,128)S(1)} %get-tuple-element.49.A_in, f32[32,144,128]{2,1,0:T(8,128)S(1)} %get-tuple-element.50.B_in, f32[24,16,128]{2,1,0:T(8,128)S(1)} %get-tuple-element.51.brate_side, f32[24,16,128]{2,1,0:T(8,128)S(1)} %get-tuple-element.52.burn_side, ...), custom_call_target="tpu_custom_call" | custom-call | tf_op jit(solution)/shard_map/outer/pallas_call | solution.py:460
Async XLA Ops:
  0.0 6.8 %copy-start.4 = (f32[64]{0:T(128)S(1)}, f32[64]{0:T(128)}, u32[]{:S(2)}) copy-start(f32[64]{0:T(128)} %param.17) | copy-start | bytes 772
  0.0 6.8 %copy-start.2 = (f32[64,64]{1,0:T(8,128)S(1)}, f32[64,64]{1,0:T(8,128)}, u32[]{:S(2)}) copy-start(f32[64,64]{1,0:T(8,128)} %react_ref.1) | copy-start | bytes 49156
  0.0 6.8 %copy-start.1 = (f32[64,64]{1,0:T(8,128)S(1)}, f32[64,64]{1,0:T(8,128)}, u32[]{:S(2)}) copy-start(f32[64,64]{1,0:T(8,128)} %cols_ref.1) | copy-start | bytes 49156
  0.0 6.8 %copy-start = (f32[64,64]{1,0:T(8,128)S(1)}, f32[64,64]{1,0:T(8,128)}, u32[]{:S(2)}) copy-start(f32[64,64]{1,0:T(8,128)} %rows_ref.1) | copy-start | bytes 49156
  0.0 6.8 %copy-start.3 = (f32[13,64]{1,0:T(8,128)S(1)}, f32[13,64]{1,0:T(8,128)}, u32[]{:S(2)}) copy-start(f32[13,64]{1,0:T(8,128)} %rate_ref.1) | copy-start | bytes 9988
  2.0 7.0 %collective-permute-start = (f32[26,8,128]{2,1,0:T(8,128)S(1)}, f32[26,8,128]{2,1,0:T(8,128)S(1)}, u32[]{:S(2)}, u32[]{:S(2)}) collective-permute-start(f32[26,8,128]{2,1,0:T(8,128)S(1)} %get-tuple-element.34), channel_id=1, source_target_pairs={{0,1},{2,3},{4,5},{6,7},{8,9},{10,11},{12,13},{14,15},{1,0},{3,2},... | collective-permute-start | bytes 319496 | tf_op jit(solution)/shard_map/ppermute | solution.py:472
  2.0 9.7 %collective-permute-start.1 = (f32[26,8,128]{2,1,0:T(8,128)S(1)}, f32[26,8,128]{2,1,0:T(8,128)S(1)}, u32[]{:S(2)}, u32[]{:S(2)}) collective-permute-start(f32[26,8,128]{2,1,0:T(8,128)S(1)} %get-tuple-element.35), channel_id=1, source_target_pairs={{1,2},{3,4},{5,6},{7,8},{9,10},{11,12},{13,14},{2,1},{4,3},{6,5},{... | collective-permute-start | bytes 319496 | tf_op jit(solution)/shard_map/ppermute | solution.py:472
  12.0 15.9 %collective-permute-start.2 = (f32[624,128]{1,0:T(8,128)S(1)}, f32[624,128]{1,0:T(8,128)S(1)}, u32[]{:S(2)}, u32[]{:S(2)}) collective-permute-start(f32[624,128]{1,0:T(8,128)S(1)} %get-tuple-element.57), channel_id=1, source_target_pairs={{0,16},{32,48},{64,80},{96,112},{16,0},{48,32},{80,64},{112,96},{1... | collective-permute-start | bytes 958472 | tf_op jit(solution)/shard_map/ppermute | solution.py:472
  12.9 15.0 %collective-permute-start.3 = (f32[624,128]{1,0:T(8,128)S(1)}, f32[624,128]{1,0:T(8,128)S(1)}, u32[]{:S(2)}, u32[]{:S(2)}) collective-permute-start(f32[624,128]{1,0:T(8,128)S(1)} %get-tuple-element.58), channel_id=1, source_target_pairs={{16,32},{48,64},{80,96},{32,16},{64,48},{96,80},{17,33},{49,65},{8... | collective-permute-start | bytes 958472 | tf_op jit(solution)/shard_map/ppermute | solution.py:472

commit v6 on v5

--- a/solution.py
+++ b/solution.py
@@ -17,6 +17,7 @@
 INNER_GROUP = 8
 OUTER_GROUP = 4
 MSG = 4 * WIDTH
+MIDDLE = COLS - 16
 BF = jnp.bfloat16
 F32 = jnp.float32
 
@@ -112,7 +113,8 @@
 
 def rates_kernel(
     masks_ref, rate_ref, heat_ref, rows_ref, cols_ref, react_ref, field_ref,
-    brate_ref, burn_ref, bheat_ref, table_ref, w1_ref, w2_ref, w3_ref, s_ref, w_ref, t_ref, tab,
+    brate_ref, burn_ref, bheat_ref, table_ref, w1_ref, w2_ref, w3_ref, s_ref, w_ref, t_ref,
+    s2_ref, w2nd_ref, t2_ref, tab,
 ):
     tab[...] = jnp.zeros_like(tab)
     tab[0:13, 0:64] = rate_ref[...]
@@ -151,6 +153,22 @@
             k, at = k0 + i, slice(i * COLS, (i + 1) * COLS)
             s_ref[k], w_ref[k] = s_all[at], w_all[at]
             t_ref[k] = 0.5 * x[at] + (burn_ref[k] * tt[at] + bheat_ref[k])
+    mid = slice(8, 8 + MIDDLE)
+
+    def s_mid(k):
+        return s_ref[k, mid] if k < OWN else pltpu.roll(s_ref[OWN - 1, mid], C, 1)
+
+    for k0, n in ((1, 7), (8, 8), (16, 8)):
+        xs = []
+        for k in range(k0, k0 + n):
+            centre = s_mid(k) + w_ref[k, mid]
+            around = (s_mid(k - 1) + s_mid(k + 1)) + (w_ref[k, 7 : 7 + MIDDLE] + w_ref[k, 9 : 9 + MIDDLE])
+            xs.append(t_ref[k, mid] + brate_ref[k, mid] * (around - centre - centre))
+        s_all, w_all, tt = mixed(jnp.concatenate(xs, 0), (w1_ref, w2_ref, w3_ref))
+        for i, x in enumerate(xs):
+            k, at = k0 + i, slice(i * MIDDLE, (i + 1) * MIDDLE)
+            s2_ref[k], w2nd_ref[k] = s_all[at], w_all[at]
+            t2_ref[k] = 0.5 * x + (burn_ref[k, mid] * tt[at] + bheat_ref[k, mid])
 
 
 def mixed(x, weights):
@@ -194,10 +212,11 @@
 
 def rates(masks, rate, heat, rows, cols, react, field):
     cells = ((OWN, COLS, LANES), F32)
+    middle = ((OWN, MIDDLE, LANES), F32)
     return call(
         rates_kernel, "rates",
         [cells, cells, cells, ((128, 384), BF), ((256, 256), BF), ((128, 256), BF), ((256, 256), BF),
-         cells, cells, cells],
+         cells, cells, cells, middle, middle, middle],
         [((16, 128), F32)],
     )(masks, rate, heat, rows, cols, react, field)
 
@@ -301,10 +320,12 @@
 
 def inner_kernel(
     field_ref, left_ref, right_ref, edge_ref, brate_in, burn_in, bheat_in, table_ref, w1, w2, w3,
-    s_in, w_in, t_in, A, B, brate, burn, bheat, kept_s, kept_w, kept_t, S, W, T, side_s, side_t, W1,
+    s_in, w_in, t_in, s2_in, w2_in, t2_in, A, B, brate, burn, bheat, kept_s, kept_w, kept_t,
+    S, W, T, side_s, side_t, W1, side2_s, side2_t, W2,
 ):
     clear_margins(W)
     clear_margins(W1)
+    clear_margins(W2)
     clear_margins(kept_w)
     for r0 in range(HALO, TILES, 8):
         put_edge_rates(edge_ref, table_ref, r0, HALO, (0, 8), brate, burn, bheat)
@@ -323,16 +344,46 @@
         W1[r, 8:16] = w_all[span][0:8]
         W1[r, 16 + COLS : 24 + COLS] = w_all[span][8:16]
 
-    def first_w(k):
-        W1[HALO + k, 16 : 16 + COLS] = w_in[k]
-
+        W1[r, 16:32] = w_in[k, 0:16]
+        W1[r, COLS : 16 + COLS] = w_in[k, COLS - 16 :]
+    W1[HALO, 16 : 16 + COLS] = w_in[0]
     s_of, t_first = beside(side_s, s_in), beside(side_t, t_in)
+    parts = (slice(0, 16), slice(COLS, WIDTH))
 
     def s_first(q):
         return s_of(q) if q < TILES else pltpu.roll(s_of(TILES - 1), C, 1)
 
-    def w_first(q, o):
-        return W1[q, o : o + WIDTH]
+    ends = []
+    for q in range(HALO + 1, TILES):
+        for at in parts:
+            a, z = at.start, at.stop
+            s_here, t_here, rate_here = s_of(q)[at], t_first(q)[at], rate[0](q)[at]
+            centre = s_here + W1[q, a + 8 : z + 8]
+            around = (s_first(q - 1)[at] + s_first(q + 1)[at]) + (W1[q, a + 7 : z + 7] + W1[q, a + 9 : z + 9])
+            ends.append(t_here + rate_here * (around - centre - centre))
+    s_all, w_all, tt = mixed(jnp.concatenate(ends, 0), (w1, w2, w3))
+    for q in range(HALO + 1, TILES):
+        k, at = q - HALO, slice(32 * (q - HALO - 1), 32 * (q - HALO))
+        x = jnp.concatenate(ends[2 * k - 2 : 2 * k], 0)
+        burn_here, bheat_here = [jnp.concatenate([rate[i](q)[p] for p in parts], 0) for i in (1, 2)]
+        side2_s[k] = s_all[at]
+        side2_t[k] = 0.5 * x + (burn_here * tt[at] + bheat_here)
+        W2[q, 8:24] = w_all[at][0:16]
+        W2[q, 8 + COLS : 24 + COLS] = w_all[at][16:32]
+
+    def second_w(k):
+        W2[HALO + k, 24 : 24 + MIDDLE] = w2_in[k]
+
+    def around_middle(side, own):
+        return lambda r: jnp.concatenate([side[r - HALO, 0:16], own[r - HALO], side[r - HALO, 16:32]], 0)
+
+    s2_of, t_second = around_middle(side2_s, s2_in), around_middle(side2_t, t2_in)
+
+    def s_second(q):
+        return s2_of(q) if q < TILES else pltpu.roll(s2_of(TILES - 1), C, 1)
+
+    def w_second(q, o):
+        return W2[q, o : o + WIDTH]
 
     A[HALO] = start(HALO)
     A[HALO + 1] = start(HALO + 1)
@@ -358,20 +409,24 @@
         )
         readers = (lambda q: S[q], lambda q, o: W[q, o : o + WIDTH], lambda q: T[q])
         if s == 1:
-            first_w(0)
-            first_w(1)
             for q in (HALO, HALO + 1):
                 keep(q, s_first(q), W1[q, 8 : 8 + WIDTH], t_first(q))
-            opening, finished = stage, [HALO + 1]
+            continue
+        if s == 2:
+            second_w(1)
+            second_w(2)
+            for q in (HALO + 1, HALO + 2):
+                keep(q, s_second(q), W2[q, 8 : 8 + WIDTH], t_second(q))
+            opening, finished = stage, [HALO + 2]
             continue
 
         def before(end):
             for q in range(finished[0], end):
-                first_w(q - HALO)
-                opening.post(q, s_first, w_first, t_first)
+                second_w(q - HALO)
+                opening.post(q, s_second, w_second, t_second)
             finished[0] = max(finished[0], end)
 
-        stage.run(TILES, *readers, keep, before if s == 2 else None)
+        stage.run(TILES, *readers, keep, before if s == 3 else None)
 
 
 def inner(field, left, right, edge, rate_arrays):
@@ -382,7 +437,8 @@
         [cells, cells, edges, edges, edges, ((STAGES, 2, WIDTH, LANES), F32),
          ((STAGES, WIDTH + 16, LANES), F32), ((STAGES, WIDTH, LANES), F32)],
         [((TILES + 1, WIDTH, LANES), F32), ((TILES, WIDTH + 16, LANES), F32), cells, edges, edges,
-         ((TILES, WIDTH + 16, LANES), F32)], limit=20,
+         ((TILES, WIDTH + 16, LANES), F32), ((OWN, 32, LANES), F32), ((OWN, 32, LANES), F32),
+         ((TILES, WIDTH + 16, LANES), F32)], limit=24,
     )(field, left, right, edge, *rate_arrays)
 
 

time: 34.8 us -> 34.2 us (0.983)
  waiting for transfers between devices: 2.83 us -> 1.64 us
  Pallas kernels: 21.5 us -> 22.1 us
    ppermute x4, waiting for transfers between devices: 2.83 us -> 1.64 us  [swap(): return lax.ppermute(x, axis, pairs + [(b, a) for a, b in pairs])]
    pallas_call x1, Pallas kernels: 2.11 us -> 3.3 us  [rates(): call(rates_kernel, 'rates', [cells, cells, cells, ((128, 384), BF), ((256...]
    pallas_call x1, Pallas kernels: 10.7 us -> 10 us  [inner(): call(inner_kernel, 'inner', [cells, cells, edges, edges, edges, ((STAGES,...]
  transfers between devices with their start and end apart: 4 -> 4, of which waited for: 1 -> 1; matrix products, arithmetic and copies ran while one was open for 0% -> 0% of each run, Pallas kernels for 37% -> 39%
where the time goes in v6:
time: 34.2 us; the launch traced here: 33.9 us
  Pallas kernels  22.1 us (65%)
  starting transfers between devices  10 us (29%)
  waiting for transfers between devices  1.64 us (5%)
    pallas_call x1, Pallas kernels, inner(): call(inner_kernel, 'inner', [cells, cells, edges, edges, edges, ((STAGES,...  10 us
    ppermute x4, starting transfers between devices, swap(): return lax.ppermute(x, axis, pairs + [(b, a) for a, b in pairs])  10 us
    pallas_call x1, Pallas kernels, outer(): call(outer_kernel, 'outer', [((C, ROWS, COLS), F32)], [cells, cells, edge...  6.66 us
    pallas_call x1, Pallas kernels, rates(): call(rates_kernel, 'rates', [cells, cells, cells, ((128, 384), BF), ((256...  3.3 us
    pallas_call x1, Pallas kernels, pack(): call(pack_kernel, 'pack', [((OWN, COLS, LANES), F32), ((256, COLS), F32),...  1.92 us
    ppermute x4, waiting for transfers between devices, swap(): return lax.ppermute(x, axis, pairs + [(b, a) for a, b in pairs])  1.64 us
  transfers between devices with their start and end apart: 4, of which 1 were waited for; matrix products, arithmetic and copies ran while one was open for 0% of the time, Pallas kernels for 39%

profile of v6, /device:TPU:104, one launch (start us, length us, event | category | flops | bytes accessed | tf_op | source)
XLA Modules:
  0.0 33.9 jit_solution(3320966135497008522)
XLA Ops:
  0.0 0.0 copy-start.4
  0.0 0.0 copy-start.2
  0.0 0.0 copy-start.1
  0.0 0.0 copy-start
  0.0 0.0 copy-start.3
  0.0 1.9 %pack.1 = (f32[24,128,128]{2,1,0:T(8,128)S(1)}, f32[256,128]{1,0:T(8,128)S(1)}, f32[26,8,128]{2,1,0:T(8,128)S(1)}, f32[26,8,128]{2,1,0:T(8,128)S(1)}) custom-call(f32[64,48,128]{2,1,0:T(8,128)} %x_hbm.1, s32[48,128]{1,0:T(8,128)} %fuel_hbm.1, s32[48,128]{1,0:T(8,128)} %break_hbm.1, s32[48,128]{1,0:T(8,128)} %lit_hbm.1), custom_call_target="tpu_custom_call" | custom-call | tf_op jit(solution)/shard_map/pack/pallas_call | solution.py:97
  2.0 0.1 collective-permute-start
  2.0 4.7 %collective-permute-start.1 = (f32[26,8,128]{2,1,0:T(8,128)S(1)}, f32[26,8,128]{2,1,0:T(8,128)S(1)}, u32[]{:S(2)}, u32[]{:S(2)}) collective-permute-start(f32[26,8,128]{2,1,0:T(8,128)S(1)} %get-tuple-element.38), channel_id=1, source_target_pairs={{1,2},{3,4},{5,6},{7,8},{9,10},{11,12},{13,14},{2,1},{4,3},{6,5},{... | collective-permute-start | bytes 319496 | tf_op jit(solution)/shard_map/ppermute | solution.py:528
  6.8 0.0 copy-done.4
  6.8 0.0 copy-done.2
  6.8 0.0 copy-done.1
  6.8 0.0 copy-done
  6.8 0.0 copy-done.3
  6.9 3.3 %rates.1 = (f32[24,128,128]{2,1,0:T(8,128)S(1)}, f32[24,128,128]{2,1,0:T(8,128)S(1)}, f32[24,128,128]{2,1,0:T(8,128)S(1)}, bf16[128,384]{1,0:T(8,128)(2,1)S(1)},...) custom-call(f32[256,128]{1,0:T(8,128)S(1)} %get-tuple-element.36.mas, ...), custom_call_target="tpu_custom_call" | custom-call | tf_op jit(solution)/shard_map/rates/pallas_call | solution.py:216
  10.2 0.0 collective-permute-done.near_ref
  10.2 1.6 %collective-permute-done.1.far_ref = f32[26,8,128]{2,1,0:T(8,128)S(1)} collective-permute-done((f32[26,8,128]{2,1,0:T(8,128)S(1)}, f32[26,8,128]{2,1,0:T(8,128)S(1)}, u32[]{:S(2)}, u32[]{:S(2)}) %collective-permute-start.1) | collective-permute-done | bytes 106528 | tf_op jit(solution)/shard_map/ppermute | solution.py:528
  11.8 0.2 rows.1
  12.0 0.5 %collective-permute-start.2 = (f32[624,128]{1,0:T(8,128)S(1)}, f32[624,128]{1,0:T(8,128)S(1)}, u32[]{:S(2)}, u32[]{:S(2)}) collective-permute-start(f32[624,128]{1,0:T(8,128)S(1)} %get-tuple-element.63), channel_id=1, source_target_pairs={{0,16},{32,48},{64,80},{96,112},{16,0},{48,32},{80,64},{112,96},{1... | collective-permute-start | bytes 958472 | tf_op jit(solution)/shard_map/ppermute | solution.py:528
  12.5 4.7 %collective-permute-start.3 = (f32[624,128]{1,0:T(8,128)S(1)}, f32[624,128]{1,0:T(8,128)S(1)}, u32[]{:S(2)}, u32[]{:S(2)}) collective-permute-start(f32[624,128]{1,0:T(8,128)S(1)} %get-tuple-element.64), channel_id=1, source_target_pairs={{16,32},{48,64},{80,96},{32,16},{64,48},{96,80},{17,33},{49,65},{8... | collective-permute-start | bytes 958472 | tf_op jit(solution)/shard_map/ppermute | solution.py:528
  17.2 10.0 %inner.1 = (f32[32,144,128]{2,1,0:T(8,128)S(1)}, f32[32,144,128]{2,1,0:T(8,128)S(1)}, f32[24,16,128]{2,1,0:T(8,128)S(1)}, f32[24,16,128]{2,1,0:T(8,128)S(1)}, f3...) custom-call(f32[24,128,128]{2,1,0:T(8,128)S(1)} %get-tuple-element.3, ...), custom_call_target="tpu_custom_call" | custom-call | tf_op jit(solution)/shard_map/inner/pallas_call | solution.py:435
  27.3 0.0 collective-permute-done.2.near_ref
  27.3 0.0 collective-permute-done.3.far_ref
  27.3 6.7 %outer.1 = f32[64,48,128]{2,1,0:T(8,128)} custom-call(f32[32,144,128]{2,1,0:T(8,128)S(1)} %get-tuple-element.55.A_in, f32[32,144,128]{2,1,0:T(8,128)S(1)} %get-tuple-element.56.B_in, f32[24,16,128]{2,1,0:T(8,128)S(1)} %get-tuple-element.57.brate_side, f32[24,16,128]{2,1,0:T(8,128)S(1)} %get-tuple-element.58.burn_side, ...), custom_call_target="tpu_custom_call" | custom-call | tf_op jit(solution)/shard_map/outer/pallas_call | solution.py:516
Async XLA Ops:
  0.0 6.8 %copy-start.4 = (f32[64]{0:T(128)S(1)}, f32[64]{0:T(128)}, u32[]{:S(2)}) copy-start(f32[64]{0:T(128)} %param.17) | copy-start | bytes 772
  0.0 6.8 %copy-start.2 = (f32[64,64]{1,0:T(8,128)S(1)}, f32[64,64]{1,0:T(8,128)}, u32[]{:S(2)}) copy-start(f32[64,64]{1,0:T(8,128)} %react_ref.1) | copy-start | bytes 49156
  0.0 6.8 %copy-start.1 = (f32[64,64]{1,0:T(8,128)S(1)}, f32[64,64]{1,0:T(8,128)}, u32[]{:S(2)}) copy-start(f32[64,64]{1,0:T(8,128)} %cols_ref.1) | copy-start | bytes 49156
  0.0 6.8 %copy-start = (f32[64,64]{1,0:T(8,128)S(1)}, f32[64,64]{1,0:T(8,128)}, u32[]{:S(2)}) copy-start(f32[64,64]{1,0:T(8,128)} %rows_ref.1) | copy-start | bytes 49156
  0.0 6.8 %copy-start.3 = (f32[13,64]{1,0:T(8,128)S(1)}, f32[13,64]{1,0:T(8,128)}, u32[]{:S(2)}) copy-start(f32[13,64]{1,0:T(8,128)} %rate_ref.1) | copy-start | bytes 9988
  2.0 8.2 %collective-permute-start = (f32[26,8,128]{2,1,0:T(8,128)S(1)}, f32[26,8,128]{2,1,0:T(8,128)S(1)}, u32[]{:S(2)}, u32[]{:S(2)}) collective-permute-start(f32[26,8,128]{2,1,0:T(8,128)S(1)} %get-tuple-element.37), channel_id=1, source_target_pairs={{0,1},{2,3},{4,5},{6,7},{8,9},{10,11},{12,13},{14,15},{1,0},{3,2},... | collective-permute-start | bytes 319496 | tf_op jit(solution)/shard_map/ppermute | solution.py:528
  2.0 9.7 %collective-permute-start.1 = (f32[26,8,128]{2,1,0:T(8,128)S(1)}, f32[26,8,128]{2,1,0:T(8,128)S(1)}, u32[]{:S(2)}, u32[]{:S(2)}) collective-permute-start(f32[26,8,128]{2,1,0:T(8,128)S(1)} %get-tuple-element.38), channel_id=1, source_target_pairs={{1,2},{3,4},{5,6},{7,8},{9,10},{11,12},{13,14},{2,1},{4,3},{6,5},{... | collective-permute-start | bytes 319496 | tf_op jit(solution)/shard_map/ppermute | solution.py:528
  12.0 15.3 %collective-permute-start.2 = (f32[624,128]{1,0:T(8,128)S(1)}, f32[624,128]{1,0:T(8,128)S(1)}, u32[]{:S(2)}, u32[]{:S(2)}) collective-permute-start(f32[624,128]{1,0:T(8,128)S(1)} %get-tuple-element.63), channel_id=1, source_target_pairs={{0,16},{32,48},{64,80},{96,112},{16,0},{48,32},{80,64},{112,96},{1... | collective-permute-start | bytes 958472 | tf_op jit(solution)/shard_map/ppermute | solution.py:528
  12.5 14.8 %collective-permute-start.3 = (f32[624,128]{1,0:T(8,128)S(1)}, f32[624,128]{1,0:T(8,128)S(1)}, u32[]{:S(2)}, u32[]{:S(2)}) collective-permute-start(f32[624,128]{1,0:T(8,128)S(1)} %get-tuple-element.64), channel_id=1, source_target_pairs={{16,32},{48,64},{80,96},{32,16},{64,48},{96,80},{17,33},{49,65},{8... | collective-permute-start | bytes 958472 | tf_op jit(solution)/shard_map/ppermute | solution.py:528

commit v7 on v6

--- a/solution.py
+++ b/solution.py
@@ -468,6 +468,13 @@
         put_rates(masks, table_ref, r, r, HALO, brate, burn, bheat)
     put_edge_rates(edge, table_ref, 0, 0, (0, HALO + COLS), brate, burn, bheat)
 
+    flat = out_ref.reshape(C * ROWS, COLS)
+
+    def put_out(k, state):
+        turned = state[HALO + k, HALO : HALO + COLS].T
+        flat[pl.ds(k, C, stride=ROWS), :] = turned[0:C]
+        flat[pl.ds(ROWS - 1 - k, C, stride=ROWS), :] = turned[C:]
+
     def reader(near, side, own):
         far = beside(side, own)
         return lambda r: near[r] if r < HALO else far(r)
@@ -501,12 +508,10 @@
             s, HALO + s, s % 2 == 0, load, old, store, rate, (w1, w2, w3), S, W, T, OUTER_GROUP
         )
         stage.run(edge_tile, s_at, w_at, t_at)
-    flat = out_ref.reshape(C * ROWS, COLS)
-    for k in reversed(range(OWN)):
-        r = HALO + k
-        turned = (A if r < 2 * HALO else A_in)[r, HALO : HALO + COLS].T
-        flat[pl.ds(k, C, stride=ROWS), :] = turned[0:C]
-        flat[pl.ds(ROWS - 1 - k, C, stride=ROWS), :] = turned[C:]
+        put_out(HALO + 2 * s - 2, A_in)
+        put_out(HALO + 2 * s - 1, A_in)
+    for k in range(HALO):
+        put_out(k, A)
 
 
 def outer(states, rate_arrays, near, far):

time: 34.2 us -> 34.1 us (level)
  no operation moved by 1% of the time
where the time goes in v7:
time: 34.1 us; the launch traced here: 33.9 us
  Pallas kernels  22.1 us (65%)
  starting transfers between devices  10 us (29%)
  waiting for transfers between devices  1.64 us (5%)
    pallas_call x1, Pallas kernels, inner(): call(inner_kernel, 'inner', [cells, cells, edges, edges, edges, ((STAGES,...  10 us
    ppermute x4, starting transfers between devices, swap(): return lax.ppermute(x, axis, pairs + [(b, a) for a, b in pairs])  10 us
    pallas_call x1, Pallas kernels, outer(): call(outer_kernel, 'outer', [((C, ROWS, COLS), F32)], [cells, cells, edge...  6.62 us
    pallas_call x1, Pallas kernels, rates(): call(rates_kernel, 'rates', [cells, cells, cells, ((128, 384), BF), ((256...  3.3 us
    pallas_call x1, Pallas kernels, pack(): call(pack_kernel, 'pack', [((OWN, COLS, LANES), F32), ((256, COLS), F32),...  1.92 us
    ppermute x4, waiting for transfers between devices, swap(): return lax.ppermute(x, axis, pairs + [(b, a) for a, b in pairs])  1.64 us
  transfers between devices with their start and end apart: 4, of which 1 were waited for; matrix products, arithmetic and copies ran while one was open for 0% of the time, Pallas kernels for 39%

profile of v7, /device:TPU:104, one launch (start us, length us, event | category | flops | bytes accessed | tf_op | source)
XLA Modules:
  0.0 33.9 jit_solution(2508054344821192180)
XLA Ops:
  0.0 0.0 copy-start.4
  0.0 0.0 copy-start.2
  0.0 0.0 copy-start.1
  0.0 0.0 copy-start
  0.0 0.0 copy-start.3
  0.0 1.9 %pack.1 = (f32[24,128,128]{2,1,0:T(8,128)S(1)}, f32[256,128]{1,0:T(8,128)S(1)}, f32[26,8,128]{2,1,0:T(8,128)S(1)}, f32[26,8,128]{2,1,0:T(8,128)S(1)}) custom-call(f32[64,48,128]{2,1,0:T(8,128)} %x_hbm.1, s32[48,128]{1,0:T(8,128)} %fuel_hbm.1, s32[48,128]{1,0:T(8,128)} %break_hbm.1, s32[48,128]{1,0:T(8,128)} %lit_hbm.1), custom_call_target="tpu_custom_call" | custom-call | tf_op jit(solution)/shard_map/pack/pallas_call | solution.py:97
  2.0 0.1 collective-permute-start
  2.0 4.7 %collective-permute-start.1 = (f32[26,8,128]{2,1,0:T(8,128)S(1)}, f32[26,8,128]{2,1,0:T(8,128)S(1)}, u32[]{:S(2)}, u32[]{:S(2)}) collective-permute-start(f32[26,8,128]{2,1,0:T(8,128)S(1)} %get-tuple-element.38), channel_id=1, source_target_pairs={{1,2},{3,4},{5,6},{7,8},{9,10},{11,12},{13,14},{2,1},{4,3},{6,5},{... | collective-permute-start | bytes 319496 | tf_op jit(solution)/shard_map/ppermute | solution.py:533
  6.8 0.0 copy-done.4
  6.8 0.0 copy-done.2
  6.8 0.0 copy-done.1
  6.8 0.0 copy-done
  6.8 0.0 copy-done.3
  6.9 3.3 %rates.1 = (f32[24,128,128]{2,1,0:T(8,128)S(1)}, f32[24,128,128]{2,1,0:T(8,128)S(1)}, f32[24,128,128]{2,1,0:T(8,128)S(1)}, bf16[128,384]{1,0:T(8,128)(2,1)S(1)},...) custom-call(f32[256,128]{1,0:T(8,128)S(1)} %get-tuple-element.36.mas, ...), custom_call_target="tpu_custom_call" | custom-call | tf_op jit(solution)/shard_map/rates/pallas_call | solution.py:216
  10.2 0.0 collective-permute-done.near_ref
  10.2 1.6 %collective-permute-done.1.far_ref = f32[26,8,128]{2,1,0:T(8,128)S(1)} collective-permute-done((f32[26,8,128]{2,1,0:T(8,128)S(1)}, f32[26,8,128]{2,1,0:T(8,128)S(1)}, u32[]{:S(2)}, u32[]{:S(2)}) %collective-permute-start.1) | collective-permute-done | bytes 106528 | tf_op jit(solution)/shard_map/ppermute | solution.py:533
  11.8 0.2 rows.1
  12.0 0.5 %collective-permute-start.2 = (f32[624,128]{1,0:T(8,128)S(1)}, f32[624,128]{1,0:T(8,128)S(1)}, u32[]{:S(2)}, u32[]{:S(2)}) collective-permute-start(f32[624,128]{1,0:T(8,128)S(1)} %get-tuple-element.63), channel_id=1, source_target_pairs={{0,16},{32,48},{64,80},{96,112},{16,0},{48,32},{80,64},{112,96},{1... | collective-permute-start | bytes 958472 | tf_op jit(solution)/shard_map/ppermute | solution.py:533
  12.5 4.7 %collective-permute-start.3 = (f32[624,128]{1,0:T(8,128)S(1)}, f32[624,128]{1,0:T(8,128)S(1)}, u32[]{:S(2)}, u32[]{:S(2)}) collective-permute-start(f32[624,128]{1,0:T(8,128)S(1)} %get-tuple-element.64), channel_id=1, source_target_pairs={{16,32},{48,64},{80,96},{32,16},{64,48},{96,80},{17,33},{49,65},{8... | collective-permute-start | bytes 958472 | tf_op jit(solution)/shard_map/ppermute | solution.py:533
  17.2 10.0 %inner.1 = (f32[32,144,128]{2,1,0:T(8,128)S(1)}, f32[32,144,128]{2,1,0:T(8,128)S(1)}, f32[24,16,128]{2,1,0:T(8,128)S(1)}, f32[24,16,128]{2,1,0:T(8,128)S(1)}, f3...) custom-call(f32[24,128,128]{2,1,0:T(8,128)S(1)} %get-tuple-element.3, ...), custom_call_target="tpu_custom_call" | custom-call | tf_op jit(solution)/shard_map/inner/pallas_call | solution.py:435
  27.3 0.0 collective-permute-done.2.near_ref
  27.3 0.0 collective-permute-done.3.far_ref
  27.3 6.6 %outer.1 = f32[64,48,128]{2,1,0:T(8,128)} custom-call(f32[32,144,128]{2,1,0:T(8,128)S(1)} %get-tuple-element.55.A_in, f32[32,144,128]{2,1,0:T(8,128)S(1)} %get-tuple-element.56.B_in, f32[24,16,128]{2,1,0:T(8,128)S(1)} %get-tuple-element.57.brate_side, f32[24,16,128]{2,1,0:T(8,128)S(1)} %get-tuple-element.58.burn_side, ...), custom_call_target="tpu_custom_call" | custom-call | tf_op jit(solution)/shard_map/outer/pallas_call | solution.py:521
Async XLA Ops:
  0.0 6.8 %copy-start.4 = (f32[64]{0:T(128)S(1)}, f32[64]{0:T(128)}, u32[]{:S(2)}) copy-start(f32[64]{0:T(128)} %param.17) | copy-start | bytes 772
  0.0 6.8 %copy-start.2 = (f32[64,64]{1,0:T(8,128)S(1)}, f32[64,64]{1,0:T(8,128)}, u32[]{:S(2)}) copy-start(f32[64,64]{1,0:T(8,128)} %react_ref.1) | copy-start | bytes 49156
  0.0 6.8 %copy-start.1 = (f32[64,64]{1,0:T(8,128)S(1)}, f32[64,64]{1,0:T(8,128)}, u32[]{:S(2)}) copy-start(f32[64,64]{1,0:T(8,128)} %cols_ref.1) | copy-start | bytes 49156
  0.0 6.8 %copy-start = (f32[64,64]{1,0:T(8,128)S(1)}, f32[64,64]{1,0:T(8,128)}, u32[]{:S(2)}) copy-start(f32[64,64]{1,0:T(8,128)} %rows_ref.1) | copy-start | bytes 49156
  0.0 6.8 %copy-start.3 = (f32[13,64]{1,0:T(8,128)S(1)}, f32[13,64]{1,0:T(8,128)}, u32[]{:S(2)}) copy-start(f32[13,64]{1,0:T(8,128)} %rate_ref.1) | copy-start | bytes 9988
  2.0 8.2 %collective-permute-start = (f32[26,8,128]{2,1,0:T(8,128)S(1)}, f32[26,8,128]{2,1,0:T(8,128)S(1)}, u32[]{:S(2)}, u32[]{:S(2)}) collective-permute-start(f32[26,8,128]{2,1,0:T(8,128)S(1)} %get-tuple-element.37), channel_id=1, source_target_pairs={{0,1},{2,3},{4,5},{6,7},{8,9},{10,11},{12,13},{14,15},{1,0},{3,2},... | collective-permute-start | bytes 319496 | tf_op jit(solution)/shard_map/ppermute | solution.py:533
  2.0 9.7 %collective-permute-start.1 = (f32[26,8,128]{2,1,0:T(8,128)S(1)}, f32[26,8,128]{2,1,0:T(8,128)S(1)}, u32[]{:S(2)}, u32[]{:S(2)}) collective-permute-start(f32[26,8,128]{2,1,0:T(8,128)S(1)} %get-tuple-element.38), channel_id=1, source_target_pairs={{1,2},{3,4},{5,6},{7,8},{9,10},{11,12},{13,14},{2,1},{4,3},{6,5},{... | collective-permute-start | bytes 319496 | tf_op jit(solution)/shard_map/ppermute | solution.py:533
  12.0 15.3 %collective-permute-start.2 = (f32[624,128]{1,0:T(8,128)S(1)}, f32[624,128]{1,0:T(8,128)S(1)}, u32[]{:S(2)}, u32[]{:S(2)}) collective-permute-start(f32[624,128]{1,0:T(8,128)S(1)} %get-tuple-element.63), channel_id=1, source_target_pairs={{0,16},{32,48},{64,80},{96,112},{16,0},{48,32},{80,64},{112,96},{1... | collective-permute-start | bytes 958472 | tf_op jit(solution)/shard_map/ppermute | solution.py:533
  12.5 14.8 %collective-permute-start.3 = (f32[624,128]{1,0:T(8,128)S(1)}, f32[624,128]{1,0:T(8,128)S(1)}, u32[]{:S(2)}, u32[]{:S(2)}) collective-permute-start(f32[624,128]{1,0:T(8,128)S(1)} %get-tuple-element.64), channel_id=1, source_target_pairs={{16,32},{48,64},{80,96},{32,16},{64,48},{96,80},{17,33},{49,65},{8... | collective-permute-start | bytes 958472 | tf_op jit(solution)/shard_map/ppermute | solution.py:533
